TPU v7x, 32 devices: a whole 2x2x4 slice. The times are simulated.
32 devices in a mesh: dp: 2 (over y), seq: 4 (over z), tensor: 4 (over x, core).
Axes of the slice: x: 2, y: 2, z: 4, core: 2. Of those that a mesh axis runs over, the one named last changes fastest.
Arguments:
- tokens: bfloat16 [8, 1500, 768], P(('dp', 'tensor'), 'seq'), may hold values from -6 to 6
- ln1_gain: bfloat16 [768], replicated, may hold values from 0.5 to 1.5
- ln1_bias: bfloat16 [768], replicated, may hold values from -3 to 3
- w_qkv: bfloat16 [3, 768, 768], P(None, None, 'tensor'), may hold values from -0.21875 to 0.21875
- b_query_value: bfloat16 [2, 768], P(None, 'tensor'), may hold values from -3 to 3
- w_out: bfloat16 [768, 768], P('tensor'), may hold values from -4 to 4
- b_out: bfloat16 [768], replicated, may hold values from -3 to 3
- ln2_gain: bfloat16 [768], replicated, may hold values from 0.5 to 1.5
- ln2_bias: bfloat16 [768], replicated, may hold values from -3 to 3
- w_up: bfloat16 [768, 3072], P(None, 'tensor'), may hold values from -0.21875 to 0.21875
- b_up: bfloat16 [3072], P('tensor'), may hold values from -3 to 3
- w_down: bfloat16 [3072, 768], P('tensor'), may hold values from -0.109375 to 0.109375
- b_down: bfloat16 [768], replicated, may hold values from -3 to 3
- cotangent: bfloat16 [8, 1500, 768], P(('dp', 'tensor'), 'seq'), may hold values from -6 to 6
Outputs:
- output: bfloat16 [8, 1500, 768], P(('dp', 'tensor'), 'seq')
- grad_tokens: bfloat16 [8, 1500, 768], P(('dp', 'tensor'), 'seq')
- grad_ln1_gain: float32 [768], P('tensor')
- grad_ln1_bias: float32 [768], P('tensor')
- grad_qkv: float32 [3, 768, 768], P(None, None, 'tensor')
- grad_qv_bias: float32 [2, 768], P(None, 'tensor')
- grad_out: float32 [768, 768], P('tensor')
- grad_out_bias: float32 [768], P('tensor')
- grad_ln2_gain: float32 [768], P('tensor')
- grad_ln2_bias: float32 [768], P('tensor')
- grad_up: float32 [768, 3072], P(None, 'tensor')
- grad_up_bias: float32 [3072], P('tensor')
- grad_down: float32 [3072, 768], P('tensor')
- grad_down_bias: float32 [768], P('tensor')
All inputs are finite; a program needn't handle non-finite values.
Results may differ from a plain program's by a relative error of at most 0.012.
Values may be sent and summed in bfloat16 or wider, within the bound.
A program may use at most 128 MiB of HBM per device.

v0:
```python
import jax
import jax.numpy as jnp
from jax import lax
from jax.sharding import PartitionSpec as P

HEAD_DIM = 64


norm_eps = 1e-05


def layer_norm(values, gain_vec, shift_vec):
    center = values - jnp.mean(values, axis=-1, keepdims=True)
    spread = jnp.mean(center * center, axis=-1, keepdims=True)
    return center * lax.rsqrt(spread + norm_eps) * gain_vec + shift_vec


def gelu_exact(values):
    return jax.nn.gelu(values, approximate=False)


def on_device(
    tokens,
    ln1_gain,
    ln1_bias,
    w_qkv,
    b_query_value,
    w_out,
    b_out,
    ln2_gain,
    ln2_bias,
    w_up,
    b_up,
    w_down,
    b_down,
    cotangent,
):
    local_width = w_qkv.shape[2]
    head_local = local_width // HEAD_DIM
    score_scale = HEAD_DIM ** (-0.5)
    float_type = jnp.float32
    resid = tokens.astype(float_type)
    gain_one = ln1_gain.astype(float_type)
    shift_one = ln1_bias.astype(float_type)
    gain_two = ln2_gain.astype(float_type)
    shift_two = ln2_bias.astype(float_type)
    norm_one = layer_norm(resid, gain_one, shift_one).astype(jnp.bfloat16)
    rows_one = lax.all_gather(norm_one, "tensor", axis=0, tiled=True)
    clip_all, span_len = (rows_one.shape[0], rows_one.shape[1])
    group_count = clip_all // 2
    projected = jnp.einsum("cfd,jde->jcfe", rows_one, w_qkv, preferred_element_type=float_type)
    bias_qv = b_query_value.astype(float_type)
    bias_three = jnp.stack([bias_qv[0], jnp.zeros_like(bias_qv[0]), bias_qv[1]])
    projected = (projected + bias_three[:, None, None, :]).astype(jnp.bfloat16)
    key_value = lax.all_gather(projected[1:3], "seq", axis=2, tiled=True)
    frame_all = key_value.shape[2]
    query_groups = projected[0].reshape(group_count, 2, span_len, head_local, HEAD_DIM)
    key_groups = key_value[0].reshape(group_count, 2, frame_all, head_local, HEAD_DIM)
    value_groups = key_value[1].reshape(group_count, 2, frame_all, head_local, HEAD_DIM)

    def attend_forward(block_in):
        query_blk, key_blk, value_blk = block_in
        scores = (
            jnp.einsum("cqhd,ckhd->chqk", query_blk, key_blk, preferred_element_type=float_type)
            * score_scale
        )
        row_top = jnp.max(scores, axis=-1, keepdims=True)
        expo_vals = jnp.exp(scores - row_top)
        denom_sum = jnp.sum(expo_vals, axis=-1, keepdims=True)
        weights = (expo_vals / denom_sum).astype(jnp.bfloat16)
        result = jnp.einsum(
            "chqk,ckhd->cqhd", weights, value_blk, preferred_element_type=float_type
        )
        return (result.astype(jnp.bfloat16), (row_top + jnp.log(denom_sum))[..., 0])

    attended_groups, log_total = lax.map(attend_forward, (query_groups, key_groups, value_groups))
    attended = attended_groups.reshape(clip_all, span_len, local_width)
    slab_rows = attended
    branch_one = lax.psum_scatter(
        jnp.einsum("cfe,ed->cfd", slab_rows, w_out, preferred_element_type=float_type),
        "tensor",
        scatter_dimension=0,
        tiled=True,
    )
    hidden = resid + branch_one + b_out.astype(float_type)
    norm_two = layer_norm(hidden, gain_two, shift_two).astype(jnp.bfloat16)
    rows_two = lax.all_gather(norm_two, "tensor", axis=0, tiled=True)
    pre_act = jnp.einsum(
        "cfd,de->cfe", rows_two, w_up, preferred_element_type=float_type
    ) + b_up.astype(float_type)
    active = gelu_exact(pre_act).astype(jnp.bfloat16)
    slab_rows = active
    branch_two = lax.psum_scatter(
        jnp.einsum("cfe,ed->cfd", slab_rows, w_down, preferred_element_type=float_type).astype(
            jnp.bfloat16
        ),
        "tensor",
        scatter_dimension=0,
        tiled=True,
    ).astype(jnp.float32)
    output = (hidden + branch_two + b_down.astype(float_type)).astype(jnp.bfloat16)
    grad_output = cotangent.astype(float_type)
    grad_rows = lax.all_gather(cotangent, "tensor", axis=0, tiled=True)
    grad_down = jnp.einsum("cfe,cfd->ed", active, grad_rows, preferred_element_type=float_type)
    grad_active = jnp.einsum("cfd,ed->cfe", grad_rows, w_down, preferred_element_type=float_type)
    gelu_value, gelu_pull = jax.vjp(gelu_exact, pre_act)
    grad_pre = gelu_pull(grad_active)[0].astype(jnp.bfloat16)
    grad_up_bias = jnp.sum(grad_pre, axis=(0, 1), dtype=float_type)
    grad_up = jnp.einsum("cfd,cfe->de", rows_two, grad_pre, preferred_element_type=float_type)
    slab_rows = grad_pre
    grad_norm_two = lax.psum_scatter(
        jnp.einsum("cfe,de->cfd", slab_rows, w_up, preferred_element_type=float_type),
        "tensor",
        scatter_dimension=0,
        tiled=True,
    )
    norm_value, norm_pull_two = jax.vjp(layer_norm, hidden, gain_two, shift_two)
    grad_hidden, grad_gain_two, grad_shift_two = norm_pull_two(grad_norm_two)
    grad_hidden = grad_hidden + grad_output
    hidden_low = grad_hidden.astype(jnp.bfloat16)
    attn_rows = lax.all_gather(hidden_low, "tensor", axis=0, tiled=True)
    grad_out = jnp.einsum("cfe,cfd->ed", attended, attn_rows, preferred_element_type=float_type)
    grad_attended = jnp.einsum(
        "cfd,ed->cfe", attn_rows, w_out, preferred_element_type=float_type
    ).astype(jnp.bfloat16)
    grad_att_groups = grad_attended.reshape(group_count, 2, span_len, head_local, HEAD_DIM)

    def attend_backward(block_in):
        query_blk, key_blk, value_blk, grad_blk, log_blk = block_in
        scores = (
            jnp.einsum("cqhd,ckhd->chqk", query_blk, key_blk, preferred_element_type=float_type)
            * score_scale
        )
        prob_rows = jnp.exp(scores - log_blk[..., None])
        grad_probs = jnp.einsum(
            "cqhd,ckhd->chqk", grad_blk, value_blk, preferred_element_type=float_type
        )
        inner_sum = jnp.sum(prob_rows * grad_probs, axis=-1, keepdims=True)
        grad_scores = (prob_rows * (grad_probs - inner_sum)).astype(jnp.bfloat16)
        grad_query = (
            jnp.einsum("chqk,ckhd->cqhd", grad_scores, key_blk, preferred_element_type=float_type)
            * score_scale
        )
        grad_key = (
            jnp.einsum("chqk,cqhd->ckhd", grad_scores, query_blk, preferred_element_type=float_type)
            * score_scale
        )
        grad_value = jnp.einsum(
            "chqk,cqhd->ckhd",
            prob_rows.astype(jnp.bfloat16),
            grad_blk,
            preferred_element_type=float_type,
        )
        return (grad_query.astype(jnp.bfloat16), grad_key, grad_value)

    grad_query, grad_key, grad_value = lax.map(
        attend_backward, (query_groups, key_groups, value_groups, grad_att_groups, log_total)
    )
    grad_key, grad_value = (
        lax.psum_scatter(
            grad_key.reshape(clip_all, frame_all, local_width),
            "seq",
            scatter_dimension=1,
            tiled=True,
        ),
        lax.psum_scatter(
            grad_value.reshape(clip_all, frame_all, local_width),
            "seq",
            scatter_dimension=1,
            tiled=True,
        ),
    )
    grad_key = grad_key.astype(jnp.bfloat16)
    grad_value = grad_value.astype(jnp.bfloat16)
    grad_query = grad_query.reshape(clip_all, span_len, local_width)
    grad_qkv_rows = jnp.stack([grad_query, grad_key, grad_value])
    grad_qv_bias = jnp.stack(
        [
            jnp.sum(grad_qkv_rows[0], axis=(0, 1), dtype=float_type),
            jnp.sum(grad_qkv_rows[2], axis=(0, 1), dtype=float_type),
        ]
    )
    grad_qkv = jnp.einsum(
        "cfd,jcfe->jde", rows_one, grad_qkv_rows, preferred_element_type=float_type
    )
    slab_rows = grad_qkv_rows
    grad_norm_one = lax.psum_scatter(
        jnp.einsum("jcfe,jde->cfd", slab_rows, w_qkv, preferred_element_type=float_type),
        "tensor",
        scatter_dimension=0,
        tiled=True,
    )
    norm_first, norm_pull_one = jax.vjp(layer_norm, resid, gain_one, shift_one)
    grad_resid, grad_gain_one, grad_shift_one = norm_pull_one(grad_norm_one)
    grad_tokens = (grad_hidden + grad_resid).astype(jnp.bfloat16)
    vector_rows = jnp.stack(
        [
            grad_gain_one,
            grad_shift_one,
            jnp.sum(grad_hidden, axis=(0, 1)),
            grad_gain_two,
            grad_shift_two,
            jnp.sum(grad_output, axis=(0, 1)),
        ]
    )
    vector_rows = lax.psum_scatter(vector_rows, "tensor", scatter_dimension=1, tiled=True)
    bundle = (grad_qkv, grad_qv_bias, grad_out, grad_up, grad_up_bias, grad_down, vector_rows)
    bundle = lax.psum(
        (bundle[0], bundle[1], bundle[2], bundle[3], bundle[4], bundle[5], bundle[6]), ("dp", "seq")
    )
    grad_qkv, grad_qv_bias, grad_out, grad_up, grad_up_bias, grad_down, vector_rows = bundle
    return (
        output,
        grad_tokens,
        vector_rows[0],
        vector_rows[1],
        grad_qkv,
        grad_qv_bias,
        grad_out,
        vector_rows[2],
        vector_rows[3],
        vector_rows[4],
        grad_up,
        grad_up_bias,
        grad_down,
        vector_rows[5],
    )


def solution(mesh):
    in_specs = (
        P(("dp", "tensor"), "seq", None),
        P(),
        P(),
        P(None, None, "tensor"),
        P(None, "tensor"),
        P("tensor", None),
        P(),
        P(),
        P(),
        P(None, "tensor"),
        P("tensor"),
        P("tensor", None),
        P(),
        P(("dp", "tensor"), "seq", None),
    )
    out_specs = (
        P(("dp", "tensor"), "seq", None),
        P(("dp", "tensor"), "seq", None),
        P("tensor"),
        P("tensor"),
        P(None, None, "tensor"),
        P(None, "tensor"),
        P("tensor", None),
        P("tensor"),
        P("tensor"),
        P("tensor"),
        P(None, "tensor"),
        P("tensor"),
        P("tensor", None),
        P("tensor"),
    )
    return jax.shard_map(
        on_device, mesh=mesh, in_specs=in_specs, out_specs=out_specs, check_vma=False
    )
```

profile of v0, /device:TPU:0, one launch (start us, length us, event | category | flops | bytes accessed | tf_op | source)
XLA Modules:
  0.0 1169.2 jit_solution(6071799092136960263)
XLA Ops:
  14.3 26.4 %all-gather.6.cloned.1.call-done = bf16[4,375,768]{2,1,0:T(8,128)(2,1)} async-done(((bf16[1,375,768]{2,1,0:T(8,128)(2,1)}), bf16[4,375,768]{2,1,0:T(8,128)(2,1)}) %all-gather.6.cloned.1.call-update) | async-done | bytes 2304016 | tf_op jit(solution)/shard_map/all_gather | solution.py:48
  49.9 111.1 %all-gather.8.cloned.1.call-done = bf16[2,4,1500,192]{3,1,0,2:T(4,128)(2,1)} async-done(((bf16[2,4,375,192]{3,1,0,2:T(4,128)(2,1)}), bf16[2,4,1500,192]{3,1,0,2:T(4,128)(2,1)}) %all-gather.8.cloned.1.call-update) | async-done | bytes 4608016 | tf_op jit(solution)/shard_map/all_gather | solution.py:55
  160.9 7.2 fusion.116
  172.5 5.7 copy.46
  179.1 47.1 %while.26 = (s32[]{:T(128)}, bf16[2,2,375,3,64]{2,4,3,1,0:T(8,128)(2,1)}, f32[2,2,3,375]{3,2,1,0:T(4,128)}, bf16[2,2,1500,3,64]{2,4,3,1,0:T(8,128)(2,1)}, bf16[2...) while((s32[]{:T(128)}, bf16[2,2,375,3,64]{2,4,3,1,0:T(8,128)(2,1)}, ...), condition=%wide.region_5.6_spmd, body=%wide.region_2.5_spmd.sunk | while | flops 894516736 | bytes 57507836 | solution.py:76
  179.1 7.9 multiply_reduce_fusion.7
  187.0 7.6 fusion.149
  194.6 6.6 fusion.150
  202.6 7.9 multiply_reduce_fusion.7
  210.5 7.6 fusion.149
  218.1 6.6 fusion.150
  231.5 44.3 %reduce-scatter.10.cloned.1.call-done = f32[1,375,768]{2,1,0:T(8,128)} async-done(((f32[4,375,768]{2,1,0:T(8,128)}), f32[1,375,768]{2,1,0:T(8,128)}) %reduce-scatter.10.cloned.1.call-update) | async-done | bytes 1152016 | tf_op jit(solution)/shard_map/reduce_scatter | solution.py:79
  281.5 22.0 %all-gather.10.cloned.1.call-done = bf16[4,375,768]{2,1,0:T(8,128)(2,1)} async-done(((bf16[1,375,768]{2,1,0:T(8,128)(2,1)}), bf16[4,375,768]{2,1,0:T(8,128)(2,1)}) %all-gather.10.cloned.1.call-update) | async-done | bytes 2304016 | tf_op jit(solution)/shard_map/all_gather | solution.py:87
  303.5 4.9 fusion.96
  310.5 11.7 %multiply_convert_fusion.1 = (bf16[4,375,768]{2,1,0:T(8,128)(2,1)}, f32[4,375,768]{2,1,0:T(8,128)}) fusion(f32[4,375,768]{2,1,0:T(8,128)S(1)} %get-tuple-element.188, f32[768]{0:T(1024)S(1)} %copy-done.47, u8[375,768]{1,0:T(8,128)(4,1)S(1)} %get-tuple-element.117, u8[375,768]{1,0:T(8,128)(4,1)S(1)} %get-tuple-element.116), kind=kLoop, calls=%fused_computation.67 | loop fusion | flops 81792000 | bytes 12099072 | tf_op jit(solution)/shard_map/convert_element_type | solution.py:91
  322.3 6.6 all-gather.12.cloned.1.call-done
  328.8 8.7 convert_reduce_fusion
  343.4 5.3 convolution_convert_fusion
  348.9 41.6 %reduce-scatter.14.cloned.1.call-done = f32[1,375,768]{2,1,0:T(8,128)} async-done(((f32[4,375,768]{2,1,0:T(8,128)}), f32[1,375,768]{2,1,0:T(8,128)}) %reduce-scatter.14.cloned.1.call-update) | async-done | bytes 1152016 | tf_op jit(solution)/shard_map/reduce_scatter | solution.py:111
  392.9 33.6 %reduce-scatter.12.cloned.1.call-done = bf16[1,375,768]{2,1,0:T(8,128)(2,1)} async-done(((bf16[4,375,768]{2,1,0:T(8,128)(2,1)}), bf16[1,375,768]{2,1,0:T(8,128)(2,1)}) %reduce-scatter.12.cloned.1.call-update) | async-done | bytes 576016 | tf_op jit(solution)/shard_map/reduce_scatter | solution.py:93
  432.7 22.6 %all-gather.14.cloned.1.call-done = bf16[4,375,768]{2,1,0:T(8,128)(2,1)} async-done(((bf16[1,375,768]{2,1,0:T(8,128)(2,1)}), bf16[4,375,768]{2,1,0:T(8,128)(2,1)}) %all-gather.14.cloned.1.call-update) | async-done | bytes 2304016 | tf_op jit(solution)/shard_map/all_gather | solution.py:121
  458.8 51.4 %while.27 = (s32[]{:T(128)}, bf16[2,2,375,3,64]{2,4,3,1,0:T(8,128)(2,1)}, f32[2,2,1500,3,64]{2,4,3,1,0:T(8,128)}, f32[2,2,1500,3,64]{2,4,3,1,0:T(8,128)}, bf16[2...) while((s32[]{:T(128)}, ...), condition=%wide.region_15.16_spmd, body=%wide.region_13.15_spmd.sunk | while | flops 2201361664 | bytes 125963584 | solution.py:156
  465.7 6.8 multiply_reduce_fusion.8
  472.5 6.9 multiply_convert_fusion.3
  491.4 6.8 multiply_reduce_fusion.8
  498.2 6.9 multiply_convert_fusion.3
  510.2 319.7 %all-reduce.9 = (bf16[4,1500,192]{1,2,0:T(8,128)(2,1)S(1)}, bf16[4,1500,192]{1,2,0:T(8,128)(2,1)}) all-reduce(f32[4,1500,192]{1,2,0:T(8,128)} %bitcast.32, f32[4,1500,192]{1,2,0:T(8,128)} %bitcast.206), channel_id=6, replica_groups=mesh['dp'=2,'seq'=4,'tensor'=4] {'seq'}, use_global_device_ids=true, to_apply=%region_17.18.clone | all-reduce | flops 2304000 | bytes 13824000
  837.6 6.0 convolution_bitcast_fusion.2
  850.2 35.1 %reduce-scatter.16.cloned.1.call-done = f32[1,375,768]{2,1,0:T(8,128)} async-done(((f32[4,375,768]{2,1,0:T(8,128)}), f32[1,375,768]{2,1,0:T(8,128)}) %reduce-scatter.16.cloned.1.call-update) | async-done | bytes 1152016 | tf_op jit(solution)/shard_map/reduce_scatter | solution.py:187
  897.5 15.0 %reduce-scatter.18.cloned.1.call-done = f32[192,6]{1,0:T(8,128)} async-done(((f32[768,6]{1,0:T(8,128)}), f32[192,6]{1,0:T(8,128)}) %reduce-scatter.18.cloned.1.call-update) | async-done | bytes 4624
  913.4 39.5 %all-reduce.2 = (f32[6,192]{1,0:T(8,128)S(1)}, f32[2,192]{1,0:T(2,128)}, f32[768]{0:T(1024)}) all-reduce(f32[6,192]{1,0:T(8,128)S(1)} %copy.45, f32[2,192]{1,0:T(2,128)S(1)} %pad_maximum_fusion.4, f32[768]{0:T(1024)S(1)} %copy-done.49), channel_id=1, replica_groups=mesh['dp'=2,'seq'=4,'tensor'=4] {'dp','seq'}, use_global_device_ids=true, to_apply=%region_28.29 | all-reduce | flops 2304 | bytes 18432 | tf_op jit(solution)/shard_map/psum | solution.py:208
  953.6 200.9 %all-reduce.8.cloned.1.call-done = (f32[3,768,192]{1,2,0:T(8,128)}, f32[192,768]{1,0:T(8,128)}, f32[768,768]{1,0:T(8,128)}, f32[768,768]{1,0:T(8,128)}) async-done(((f32[3,768,192]{1,2,0:T(8,128)}, f32[192,768]{1,0:T(8,128)}, f32[768,768]{1,0:T(8,128)}, f32[768,768]{1,0:T(8,128)}), (f32[3,768,192]{1,2,0:T(8,128)}, f32[192,768]{1,0:T(8,128)}, f32[768,768]{1,0:T(8,128)}, ...) | async-done | bytes 7077904 | tf_op jit(solution)/shard_map/psum | solution.py:208
  (235 shorter events, 113.9 us)
Async XLA Ops:
  7.2 296.3 %copy-start = (bf16[768,768]{1,0:T(8,128)(2,1)S(1)}, bf16[768,768]{1,0:T(8,128)(2,1)}, u32[]{:S(2)}) copy-start(bf16[768,768]{1,0:T(8,128)(2,1)} %param.27) | copy-start | bytes 3538948
  7.2 7.0 copy-start.50
  7.2 33.5 %copy-start.56 = (bf16[3,768,192]{1,2,0:T(8,128)(2,1)S(1)}, bf16[3,768,192]{1,2,0:T(8,128)(2,1)}, u32[]{:S(2)}) copy-start(bf16[3,768,192]{1,2,0:T(8,128)(2,1)} %param.21) | copy-start | bytes 2654212
  7.2 33.5 %all-gather.6.cloned.1.call-start = ((), (), s32[]{:S(2)}) async-start(), calls=%async_computation.5 | async-start | bytes 2887680 | tf_op jit(solution)/shard_map/all_gather | solution.py:48
  14.1 146.8 %all-gather.8.cloned.1.call-start = ((), (), s32[]{:S(2)}) async-start(), calls=%async_computation.6 | async-start | bytes 7680000 | tf_op jit(solution)/shard_map/all_gather | solution.py:55
  47.9 227.9 %reduce-scatter.10.cloned.1.call-start = ((), (), s32[]{:S(2)}) async-start(), calls=%async_computation.7 | async-start | bytes 5775360 | tf_op jit(solution)/shard_map/reduce_scatter | solution.py:79
  187.0 7.6 copy-start.3
  187.0 7.6 copy-start.21
  210.5 7.6 copy-start.3
  210.5 7.6 copy-start.21
  230.2 73.3 %all-gather.10.cloned.1.call-start = ((), (), s32[]{:S(2)}) async-start(), calls=%async_computation.8 | async-start | bytes 2887680 | tf_op jit(solution)/shard_map/all_gather | solution.py:87
  279.6 49.3 %all-gather.12.cloned.1.call-start = ((), (), s32[]{:S(2)}) async-start(), calls=%async_computation.10 | async-start | bytes 2887680 | tf_op jit(solution)/shard_map/all_gather | solution.py:103
  280.1 110.4 %reduce-scatter.14.cloned.1.call-start = ((), (), s32[]{:S(2)}) async-start(), calls=%async_computation.11 | async-start | bytes 5775360 | tf_op jit(solution)/shard_map/reduce_scatter | solution.py:111
  303.5 7.0 copy-start.47
  343.2 83.3 %reduce-scatter.12.cloned.1.call-start = ((), (), s32[]{:S(2)}) async-start(), calls=%async_computation.9 | async-start | bytes 2887680 | tf_op jit(solution)/shard_map/reduce_scatter | solution.py:93
  348.8 41.7 %copy-start.6 = (f32[1,375,768]{2,1,0:T(8,128)S(1)}, f32[1,375,768]{2,1,0:T(8,128)}, u32[]{:S(2)}) copy-start(f32[1,375,768]{2,1,0:T(8,128)} %copy-done.5) | copy-start | bytes 3456004
  348.8 106.5 %all-gather.14.cloned.1.call-start = ((), (), s32[]{:S(2)}) async-start(), calls=%async_computation.12 | async-start | bytes 2887680 | tf_op jit(solution)/shard_map/all_gather | solution.py:121
  431.3 27.5 %copy-start.2 = (bf16[2,2,375,3,64]{2,4,3,1,0:T(8,128)(2,1)S(1)}, bf16[2,2,375,3,64]{2,4,3,1,0:T(8,128)(2,1)}, u32[]{:S(2)}) copy-start(bf16[2,2,375,3,64]{2,4,3,1,0:T(8,128)(2,1)} %get-tuple-element.377) | copy-start | bytes 1728004
  431.3 453.9 %reduce-scatter.16.cloned.1.call-start = ((), (), s32[]{:S(2)}) async-start(), calls=%async_computation.13 | async-start | bytes 5775360 | tf_op jit(solution)/shard_map/reduce_scatter | solution.py:187
  472.5 6.9 copy-start.17
  829.9 7.6 copy-start.31
  837.5 75.0 %reduce-scatter.18.cloned.1.call-start = ((), (), s32[]{:S(2)}) async-start(), calls=%async_computation.14 | async-start | bytes 491520
  847.2 38.0 %copy-start.7 = (bf16[1,375,768]{2,1,0:T(8,128)(2,1)S(1)}, bf16[1,375,768]{2,1,0:T(8,128)(2,1)}, u32[]{:S(2)}) copy-start(bf16[1,375,768]{2,1,0:T(8,128)(2,1)} %param.18) | copy-start | bytes 1728004
  847.2 38.0 %copy-start.36 = (f32[768]{0:T(1024)S(1)}, f32[768]{0:T(1024)}, u32[]{:S(2)}) copy-start(f32[768]{0:T(1024)} %copy-done.35) | copy-start | bytes 9220
  847.2 38.0 %copy-start.38 = (f32[375]{0:T(512)S(1)}, f32[375]{0:T(512)}, u32[]{:S(2)}) copy-start(f32[375]{0:T(512)} %copy-done.37) | copy-start | bytes 4504
  847.3 39.8 %copy-start.44 = (f32[375]{0:T(512)S(1)}, f32[375]{0:T(512)}, u32[]{:S(2)}) copy-start(f32[375]{0:T(512)} %copy-done.43) | copy-start | bytes 4504
  847.3 39.8 %copy-start.40 = (f32[375]{0:T(512)S(1)}, f32[375]{0:T(512)}, u32[]{:S(2)}) copy-start(f32[375]{0:T(512)} %copy-done.39) | copy-start | bytes 4504
  850.2 38.7 %copy-start.9 = (f32[1,375,768]{2,1,0:T(8,128)S(1)}, f32[1,375,768]{2,1,0:T(8,128)}, u32[]{:S(2)}) copy-start(f32[1,375,768]{2,1,0:T(8,128)} %copy-done.8) | copy-start | bytes 3456004
  850.2 38.7 %copy-start.13 = (bf16[1,375,768]{2,1,0:T(8,128)(2,1)S(1)}, bf16[1,375,768]{2,1,0:T(8,128)(2,1)}, u32[]{:S(2)}) copy-start(bf16[1,375,768]{2,1,0:T(8,128)(2,1)} %param.31) | copy-start | bytes 1728004
  850.2 38.8 %copy-start.42 = (f32[375]{0:T(512)S(1)}, f32[375]{0:T(512)}, u32[]{:S(2)}) copy-start(f32[375]{0:T(512)} %copy-done.41) | copy-start | bytes 4504
  891.5 263.1 %all-reduce.8.cloned.1.call-start = ((), (), s32[]{:S(2)}) async-start(), calls=%async_computation.15 | async-start | bytes 14155776 | tf_op jit(solution)/shard_map/psum | solution.py:208
  894.7 18.8 %copy-start.49 = (f32[768]{0:T(1024)S(1)}, f32[768]{0:T(1024)}, u32[]{:S(2)}) copy-start(f32[768]{0:T(1024)} %get-tuple-element.189) | copy-start | bytes 9220
  (46 other events, 126.2 us)
Sparse Core Ops, SparseCore 0:
  14.2 26.4 all-gather.5
  48.0 112.9 all-gather.7
  230.3 45.4 reduce-scatter.9
  279.7 23.7 all-gather.9
  305.0 23.7 all-gather.11
  343.3 47.1 reduce-scatter.13
  393.7 32.7 reduce-scatter.11
  431.4 23.8 all-gather.13
  837.6 47.5 reduce-scatter.15
  891.6 20.8 reduce-scatter.17
  918.1 236.4 all-reduce.7
where the time goes:
time: 1180 us; the launch traced here: 1170 us
  waiting for transfers between devices  560 us (47%)
  blocking collectives  359 us (30%)
  matrix products  118 us (10%)
  other arithmetic  64.8 us (5%)
  local copies, waits for them, and re-layouts  50.8 us (4%)
  between operations  15.4 us (1%)
    unnamed x1, blocking collectives  320 us
    psum x1, waiting for transfers between devices, on_device(): lax.psum((bundle[0], bundle[1], bundle[2], bundle[3], bundle[4], bundle[5...  201 us
    all_gather x1, waiting for transfers between devices, on_device(): key_value = lax.all_gather(projected[1:3], 'seq', axis=2, tiled=True)  111 us
    reduce_scatter x1, waiting for transfers between devices, on_device(): lax.psum_scatter(jnp.einsum('cfe,ed->cfd', slab_rows, w_out, preferred_el...  44.3 us
    reduce_scatter x1, waiting for transfers between devices, on_device(): lax.psum_scatter(jnp.einsum('cfe,de->cfd', slab_rows, w_up, preferred_ele...  41.6 us
    psum x1, blocking collectives, on_device(): lax.psum((bundle[0], bundle[1], bundle[2], bundle[3], bundle[4], bundle[5...  39.5 us
    reduce_scatter x1, waiting for transfers between devices, on_device(): lax.psum_scatter(jnp.einsum('jcfe,jde->cfd', slab_rows, w_qkv, preferred_...  35.1 us
    reduce_scatter x1, waiting for transfers between devices, on_device(): lax.psum_scatter(jnp.einsum('cfe,ed->cfd', slab_rows, w_down, preferred_e...  33.6 us
  transfers between devices with their start and end apart: 11, of which 11 were waited for; matrix products, arithmetic and copies ran while one was open for 4% of the time, Pallas kernels for 0%

commit v1 on v0

v1 whole, which is shorter than its diff:
```python
import functools

import jax
import jax.numpy as jnp
from jax import lax
from jax.experimental import pallas as pl
from jax.experimental.pallas import tpu as pltpu
from jax.sharding import PartitionSpec as P

HEAD_DIM = 64
norm_eps = 1e-05
MESH = pl.DeviceIdType.MESH
PIECES = 4
VMEM_BYTES = 56 * 1024 * 1024
F32 = jnp.float32
BF16 = jnp.bfloat16


def greet(axis, peers):
    barrier = pltpu.get_barrier_semaphore()
    for peer in peers:
        pl.semaphore_signal(barrier, inc=1, device_id={axis: peer}, device_id_type=MESH)
    pl.semaphore_wait(barrier, len(peers))


def remote(axis, src, dst, send, recv, peer):
    copy = pltpu.make_async_remote_copy(
        src_ref=src,
        dst_ref=dst,
        send_sem=send,
        recv_sem=recv,
        device_id={axis: peer},
        device_id_type=MESH,
    )
    copy.start()
    return copy


def tensor_peers():
    me = lax.axis_index("tensor")
    near = me + 1 - 2 * lax.rem(me, 2)
    far = lax.rem(me + 2, 4)
    corner = lax.rem(near + 2, 4)
    return me, near, far, corner


def gather_kernel(x_ref, o_ref, own_sem, far_send, far_recv, near_send, near_recv, pass_send, pass_recv):
    me, near, far, _ = tensor_peers()
    step = x_ref.shape[0] // PIECES
    greet("tensor", (near, far))
    far_copies = []
    for piece in range(PIECES):
        span = pl.ds(piece * step, step)
        far_copies.append(
            remote("tensor", x_ref.at[span], o_ref.at[me, span], far_send.at[piece], far_recv.at[piece], far)
        )
    near_copy = remote("tensor", x_ref, o_ref.at[me], near_send, near_recv, near)
    own = pltpu.make_async_copy(x_ref, o_ref.at[me], own_sem)
    own.start()
    passed = []
    for piece in range(PIECES):
        span = pl.ds(piece * step, step)
        far_copies[piece].wait_recv()
        passed.append(
            remote(
                "tensor", o_ref.at[far, span], o_ref.at[far, span], pass_send.at[piece], pass_recv.at[piece], near
            )
        )
    own.wait()
    near_copy.wait()
    for piece in range(PIECES):
        far_copies[piece].wait_send()
        passed[piece].wait()


def gather_rows(block):
    return pl.pallas_call(
        gather_kernel,
        out_shape=jax.ShapeDtypeStruct((4,) + block.shape, block.dtype),
        in_specs=[pl.BlockSpec(memory_space=pl.ANY)],
        out_specs=pl.BlockSpec(memory_space=pl.ANY),
        scratch_shapes=[
            pltpu.SemaphoreType.DMA,
            pltpu.SemaphoreType.DMA((PIECES,)),
            pltpu.SemaphoreType.DMA((PIECES,)),
            pltpu.SemaphoreType.DMA,
            pltpu.SemaphoreType.DMA,
            pltpu.SemaphoreType.DMA((PIECES,)),
            pltpu.SemaphoreType.DMA((PIECES,)),
        ],
        compiler_params=pltpu.CompilerParams(
            collective_id=0, has_side_effects=True, vmem_limit_bytes=VMEM_BYTES
        ),
        name="gather_rows",
    )(block)


def scatter_kernel(
    x_ref, o_ref, got_far, got_own, mixed, got_sum, a_send, a_recv, b_send, b_recv, c_send, c_recv
):
    me, near, far, corner = tensor_peers()
    step = x_ref.shape[1] // PIECES
    greet("tensor", (near, far))
    spans = [pl.ds(piece * step, step) for piece in range(PIECES)]
    first = [
        remote("tensor", x_ref.at[corner, span], got_far.at[span], a_send.at[i], a_recv.at[i], near)
        for i, span in enumerate(spans)
    ]
    second = remote("tensor", x_ref.at[near], got_own, b_send, b_recv, near)
    third = []
    for i, span in enumerate(spans):
        first[i].wait_recv()
        mixed[span] = (x_ref[far, span].astype(F32) + got_far[span].astype(F32)).astype(BF16)
        third.append(remote("tensor", mixed.at[span], got_sum.at[span], c_send.at[i], c_recv.at[i], far))
    second.wait_recv()
    for i, span in enumerate(spans):
        third[i].wait_recv()
        o_ref[span] = x_ref[me, span].astype(F32) + got_own[span].astype(F32) + got_sum[span].astype(F32)
    second.wait_send()
    for i in range(PIECES):
        first[i].wait_send()
        third[i].wait_send()


def scatter_sum(blocks):
    shape = blocks.shape[1:]
    return pl.pallas_call(
        scatter_kernel,
        out_shape=jax.ShapeDtypeStruct(shape, F32),
        in_specs=[pl.BlockSpec(memory_space=pltpu.VMEM)],
        out_specs=pl.BlockSpec(memory_space=pltpu.VMEM),
        scratch_shapes=[pltpu.VMEM(shape, BF16)] * 4
        + [
            pltpu.SemaphoreType.DMA((PIECES,)),
            pltpu.SemaphoreType.DMA((PIECES,)),
            pltpu.SemaphoreType.DMA,
            pltpu.SemaphoreType.DMA,
            pltpu.SemaphoreType.DMA((PIECES,)),
            pltpu.SemaphoreType.DMA((PIECES,)),
        ],
        compiler_params=pltpu.CompilerParams(
            collective_id=1, has_side_effects=True, vmem_limit_bytes=VMEM_BYTES
        ),
        name="scatter_sum",
    )(blocks)


def swap_kernel(x_ref, o_ref, own_sem, send, recv):
    me = lax.axis_index("seq")
    peers = [lax.rem(me + hop, 4) for hop in (2, 1, 3)]
    greet("seq", peers)
    copies = [
        remote("seq", x_ref.at[peer], o_ref.at[me], send.at[i], recv.at[i], peer)
        for i, peer in enumerate(peers)
    ]
    own = pltpu.make_async_copy(x_ref.at[me], o_ref.at[me], own_sem)
    own.start()
    own.wait()
    for copy in copies:
        copy.wait()


def swap_seq(blocks, ident):
    return pl.pallas_call(
        swap_kernel,
        out_shape=jax.ShapeDtypeStruct(blocks.shape, blocks.dtype),
        in_specs=[pl.BlockSpec(memory_space=pl.ANY)],
        out_specs=pl.BlockSpec(memory_space=pl.ANY),
        scratch_shapes=[
            pltpu.SemaphoreType.DMA,
            pltpu.SemaphoreType.DMA((3,)),
            pltpu.SemaphoreType.DMA((3,)),
        ],
        compiler_params=pltpu.CompilerParams(
            collective_id=ident, has_side_effects=True, vmem_limit_bytes=VMEM_BYTES
        ),
        name="swap_seq",
    )(blocks)


def rows_dot(a, b):
    return lax.dot_general(a, b, (((0,), (0,)), ((), ())), preferred_element_type=F32)


def cols_dot(a, b):
    return lax.dot_general(a, b, (((1,), (1,)), ((), ())), preferred_element_type=F32)


def side_by_side(ref):
    return jnp.concatenate([ref[i, 0] for i in range(ref.shape[0])], axis=1)


def masked_scores(key_cols, query_cols, span, real):
    scores = rows_dot(key_cols, query_cols)
    row = lax.broadcasted_iota(jnp.int32, (scores.shape[0], 1), 0)
    return jnp.where(lax.rem(row, span) < real, scores, -1e30)


def attend_kernel(real, q_ref, k_ref, v_ref, o_ref, lse_ref):
    shards, _, _, span = q_ref.shape
    key_cols, value_cols = side_by_side(k_ref), side_by_side(v_ref)
    for i in range(shards):
        scores = masked_scores(key_cols, q_ref[i, 0], span, real)
        top = jnp.max(scores, axis=0, keepdims=True)
        expo = jnp.exp(scores - top)
        total = jnp.sum(expo, axis=0, keepdims=True)
        probs = (expo * (1.0 / total)).astype(BF16)
        o_ref[i, 0] = jnp.dot(value_cols, probs, preferred_element_type=F32).astype(BF16)
        lse_ref[i, 0] = top + jnp.log(total)


def head_spec(shards, span, offset):
    return pl.BlockSpec((shards, 1, HEAD_DIM, span), lambda h: (0, offset + h, 0, 0))


def attend_forward(qkv, heads, real):
    shards, _, _, span = qkv.shape
    return pl.pallas_call(
        functools.partial(attend_kernel, real),
        grid=(heads,),
        out_shape=(
            jax.ShapeDtypeStruct((shards, heads, HEAD_DIM, span), BF16),
            jax.ShapeDtypeStruct((shards, heads, 1, span), F32),
        ),
        in_specs=[head_spec(shards, span, 0), head_spec(shards, span, heads), head_spec(shards, span, 2 * heads)],
        out_specs=(
            head_spec(shards, span, 0),
            pl.BlockSpec((shards, 1, 1, span), lambda h: (0, h, 0, 0)),
        ),
        compiler_params=pltpu.CompilerParams(vmem_limit_bytes=VMEM_BYTES),
        name="attend_forward",
    )(qkv, qkv, qkv)


def attend_back_kernel(real, q_ref, k_ref, v_ref, g_ref, lse_ref, dq_ref, dk_ref, dv_ref):
    shards, _, _, span = q_ref.shape
    key_cols, value_cols = side_by_side(k_ref), side_by_side(v_ref)
    grad_key, grad_value = None, None
    for i in range(shards):
        query, grad = q_ref[i, 0], g_ref[i, 0]
        scores = masked_scores(key_cols, query, span, real)
        probs = jnp.exp(scores - lse_ref[i, 0])
        grad_probs = rows_dot(value_cols, grad)
        inner = jnp.sum(probs * grad_probs, axis=0, keepdims=True)
        grad_scores = (probs * (grad_probs - inner)).astype(BF16)
        dq_ref[i, 0] = (
            jnp.dot(key_cols, grad_scores, preferred_element_type=F32) * HEAD_DIM ** (-0.5)
        ).astype(BF16)
        key_part = cols_dot(query, grad_scores)
        value_part = cols_dot(grad, probs.astype(BF16))
        grad_key = key_part if grad_key is None else grad_key + key_part
        grad_value = value_part if grad_value is None else grad_value + value_part
    for i in range(shards):
        dk_ref[i, 0] = grad_key[:, i * span : (i + 1) * span].astype(BF16)
        dv_ref[i, 0] = grad_value[:, i * span : (i + 1) * span].astype(BF16)


def attend_backward(qkv, grad, lse, heads, real):
    shards, _, _, span = qkv.shape
    lse_spec = pl.BlockSpec((shards, 1, 1, span), lambda h: (0, h, 0, 0))
    shape = jax.ShapeDtypeStruct((shards, heads, HEAD_DIM, span), BF16)
    return pl.pallas_call(
        functools.partial(attend_back_kernel, real),
        grid=(heads,),
        out_shape=(shape, shape, shape),
        in_specs=[
            head_spec(shards, span, 0),
            head_spec(shards, span, heads),
            head_spec(shards, span, 2 * heads),
            head_spec(shards, span, 0),
            lse_spec,
        ],
        out_specs=(head_spec(shards, span, 0),) * 3,
        compiler_params=pltpu.CompilerParams(vmem_limit_bytes=VMEM_BYTES),
        name="attend_backward",
    )(qkv, qkv, qkv, grad, lse)


def project_kernel(rows_ref, w_ref, b_ref, o_ref):
    total = cols_dot(w_ref[...], rows_ref[0]) + b_ref[...]
    width = total.shape[0] // 3
    o_ref[0, :width] = (total[:width].astype(BF16).astype(F32) * HEAD_DIM ** (-0.5)).astype(BF16)
    o_ref[0, width:] = total[width:].astype(BF16)


def project(rows, w_flat, bias):
    clips, span, depth = rows.shape
    width = w_flat.shape[0]
    return pl.pallas_call(
        project_kernel,
        grid=(clips,),
        out_shape=jax.ShapeDtypeStruct((clips, width, span), BF16),
        in_specs=[
            pl.BlockSpec((1, span, depth), lambda c: (c, 0, 0)),
            pl.BlockSpec((width, depth), lambda c: (0, 0)),
            pl.BlockSpec((width, 1), lambda c: (0, 0)),
        ],
        out_specs=pl.BlockSpec((1, width, span), lambda c: (c, 0, 0)),
        compiler_params=pltpu.CompilerParams(vmem_limit_bytes=VMEM_BYTES),
        name="project",
    )(rows, w_flat, bias)


def layer_norm(values, gain_vec, shift_vec):
    center = values - jnp.mean(values, axis=-1, keepdims=True)
    spread = jnp.mean(center * center, axis=-1, keepdims=True)
    return center * lax.rsqrt(spread + norm_eps) * gain_vec + shift_vec


def gelu_exact(values):
    return jax.nn.gelu(values, approximate=False)


def dot(spec, a, b):
    return jnp.einsum(spec, a, b, preferred_element_type=F32)


def on_device(
    tokens,
    ln1_gain,
    ln1_bias,
    w_qkv,
    b_query_value,
    w_out,
    b_out,
    ln2_gain,
    ln2_bias,
    w_up,
    b_up,
    w_down,
    b_down,
    cotangent,
):
    width = w_qkv.shape[2]
    depth = w_qkv.shape[1]
    heads = width // HEAD_DIM
    real = tokens.shape[1]
    span = -(-real // 128) * 128
    pad = ((0, span - real), (0, 0))
    resid = jnp.pad(tokens[0], pad).astype(F32)
    cot = jnp.pad(cotangent[0], pad)
    gain_one, shift_one = ln1_gain.astype(F32), ln1_bias.astype(F32)
    gain_two, shift_two = ln2_gain.astype(F32), ln2_bias.astype(F32)
    norm_one = layer_norm(resid, gain_one, shift_one).astype(BF16)
    rows_one = gather_rows(norm_one)
    clips = rows_one.shape[0]
    w_flat = jnp.swapaxes(w_qkv, 1, 2).reshape(3 * width, depth)
    bias_qv = b_query_value.astype(F32)
    bias_three = jnp.concatenate([bias_qv[0], jnp.zeros_like(bias_qv[0]), bias_qv[1]])[:, None]
    projected = project(rows_one, w_flat, bias_three)
    qkv = swap_seq(projected, 2).reshape(clips, 3 * heads, HEAD_DIM, span)
    attended, lse = attend_forward(qkv, heads, real)
    attended = swap_seq(attended.reshape(clips, width, span), 3)
    branch_one = scatter_sum(dot("cef,ed->cfd", attended, w_out).astype(BF16))
    hidden = resid + branch_one + b_out.astype(F32)
    norm_two = layer_norm(hidden, gain_two, shift_two).astype(BF16)
    rows_two = gather_rows(norm_two)
    cot_rows = lax.all_gather(cot, "tensor", axis=0, tiled=False)
    pre_act = dot("cfd,de->cfe", rows_two, w_up) + b_up.astype(F32)
    active = gelu_exact(pre_act).astype(BF16)
    grad_active = dot("cfd,ed->cfe", cot_rows, w_down)
    _, gelu_pull = jax.vjp(gelu_exact, pre_act)
    grad_pre = gelu_pull(grad_active)[0].astype(BF16)
    grad_norm_two = dot("cfe,de->cfd", grad_pre, w_up).astype(BF16)
    branch_two = lax.psum_scatter(
        dot("cfe,ed->cfd", active, w_down).astype(BF16), "tensor", scatter_dimension=0, tiled=False
    ).astype(F32)
    output = (hidden + branch_two + b_down.astype(F32)).astype(BF16)
    grad_down = dot("cfe,cfd->ed", active, cot_rows)
    grad_up_bias = jnp.sum(grad_pre, axis=(0, 1), dtype=F32)
    grad_up = dot("cfd,cfe->de", rows_two, grad_pre)
    grad_up, grad_down, grad_norm_two = lax.optimization_barrier(
        (grad_up.astype(BF16), grad_down.astype(BF16), grad_norm_two)
    )
    grad_up, grad_down = lax.psum((grad_up, grad_down), ("dp", "seq"))
    grad_norm_two = scatter_sum(grad_norm_two)

    _, pull_two = jax.vjp(layer_norm, hidden, gain_two, shift_two)
    grad_hidden, grad_gain_two, grad_shift_two = pull_two(grad_norm_two)
    grad_hidden = grad_hidden + cot.astype(F32)
    hidden_low = grad_hidden.astype(BF16)
    grad_rows = gather_rows(hidden_low)
    grad_att = dot("cfd,ed->cef", grad_rows, w_out).astype(BF16)
    grad_out = dot("cef,cfd->ed", attended, grad_rows)
    grad_att = swap_seq(grad_att, 3).reshape(clips, heads, HEAD_DIM, span)
    grads = attend_backward(qkv, grad_att, lse, heads, real)
    grad_qkv_cols = jnp.concatenate([g.reshape(clips, width, span) for g in grads], axis=1)
    grad_qkv_cols = swap_seq(grad_qkv_cols, 2)
    grad_norm_one = scatter_sum(dot("ckf,kd->cfd", grad_qkv_cols, w_flat).astype(BF16))
    bias_sums = jnp.sum(grad_qkv_cols, axis=(0, 2), dtype=F32).reshape(3, width)
    grad_qkv = dot("cfd,ckf->dk", rows_one, grad_qkv_cols)
    grad_qkv, grad_out = grad_qkv.astype(BF16), grad_out.astype(BF16)
    grad_qkv, grad_out = lax.psum((grad_qkv, grad_out), ("seq", "dp"))
    grad_qkv = jnp.swapaxes(grad_qkv.reshape(depth, 3, width), 0, 1).astype(F32)

    _, pull_one = jax.vjp(layer_norm, resid, gain_one, shift_one)
    grad_resid, grad_gain_one, grad_shift_one = pull_one(grad_norm_one)
    grad_tokens = (grad_hidden + grad_resid).astype(BF16)
    vectors = jnp.stack(
        [
            grad_gain_one,
            grad_shift_one,
            jnp.sum(grad_hidden, axis=0),
            grad_gain_two,
            grad_shift_two,
            jnp.sum(cot.astype(F32), axis=0),
        ]
    )
    me = lax.axis_index("tensor")
    parts = lax.axis_size("tensor")
    local = jnp.concatenate([bias_sums[0], bias_sums[2], grad_up_bias])
    placed = jnp.where(jnp.arange(parts)[:, None] == me, local[None], 0.0)
    flat = lax.psum(jnp.concatenate([vectors.reshape(-1), placed.reshape(-1)]), ("dp", "seq", "tensor"))
    vectors = lax.dynamic_slice_in_dim(flat[: vectors.size].reshape(vectors.shape), me * width, width, 1)
    local = lax.dynamic_slice_in_dim(flat[vectors.shape[0] * depth :].reshape(parts, -1), me, 1, 0)[0]
    return (
        output[None, :real],
        grad_tokens[None, :real],
        vectors[0],
        vectors[1],
        grad_qkv,
        local[: 2 * width].reshape(2, width),
        grad_out.astype(F32),
        vectors[2],
        vectors[3],
        vectors[4],
        grad_up.astype(F32),
        local[2 * width :],
        grad_down.astype(F32),
        vectors[5],
    )


def solution(mesh):
    in_specs = (
        P(("dp", "tensor"), "seq", None),
        P(),
        P(),
        P(None, None, "tensor"),
        P(None, "tensor"),
        P("tensor", None),
        P(),
        P(),
        P(),
        P(None, "tensor"),
        P("tensor"),
        P("tensor", None),
        P(),
        P(("dp", "tensor"), "seq", None),
    )
    out_specs = (
        P(("dp", "tensor"), "seq", None),
        P(("dp", "tensor"), "seq", None),
        P("tensor"),
        P("tensor"),
        P(None, None, "tensor"),
        P(None, "tensor"),
        P("tensor", None),
        P("tensor"),
        P("tensor"),
        P("tensor"),
        P(None, "tensor"),
        P("tensor"),
        P("tensor", None),
        P("tensor"),
    )
    return jax.shard_map(
        on_device, mesh=mesh, in_specs=in_specs, out_specs=out_specs, check_vma=False
    )
```

time: 1180 us -> 592 us (0.50)
  waiting for transfers between devices: 560 us -> 146 us
  blocking collectives: 359 us -> 48.4 us
  Pallas kernels: 0 us -> 282 us
  matrix products: 118 us -> 45 us
  local copies, waits for them, and re-layouts: 50.8 us -> 9.72 us
  other arithmetic: 64.8 us -> 36.6 us
    unnamed x1 -> x0, blocking collectives: 320 us -> none
    pallas_call x0 -> x13, Pallas kernels: none -> 282 us  [the longest x4 108 us: swap_seq(): pl.pallas_call(swap_kernel, out_shape=jax.ShapeDtypeStruct(blocks.shape,...]
    all_gather x5 -> x1, waiting for transfers between devices: 189 us -> 0.01 us  [on_device(): cot_rows = lax.all_gather(cot, 'tensor', axis=0, tiled=False)]
    reduce_scatter x4 -> x1, waiting for transfers between devices: 155 us -> 32.2 us  [on_device(): lax.psum_scatter(dot('cfe,ed->cfd', active, w_down).astype(BF16), 'tensor...]
    psum x1 -> x2, waiting for transfers between devices: 201 us -> 113 us  [the longest x1 111 us: on_device(): grad_up, grad_down = lax.psum((grad_up, grad_down), ('dp', 'seq'))]
    dot_general x26 -> x11, matrix products: 118 us -> 45 us  [dot(): return jnp.einsum(spec, a, b, preferred_element_type=F32)]
    unnamed x111 -> x58, local copies, waits for them, and re-layouts: 29.8 us -> 4.6 us
    reduce_sum x5 -> x2, other arithmetic: 18.2 us -> 0.58 us  [the longest x1 0.32 us: on_device(): bias_sums = jnp.sum(grad_qkv_cols, axis=(0, 2), dtype=F32).reshape(3, width)]
  transfers between devices with their start and end apart: 11 -> 4, of which waited for: 11 -> 3; matrix products, arithmetic and copies ran while one was open for 4% -> 8% of each run, Pallas kernels for 0% -> 28%
where the time goes in v1:
time: 592 us; the launch traced here: 582 us
  Pallas kernels  282 us (48%)
  waiting for transfers between devices  146 us (25%)
  blocking collectives  48.4 us (8%)
  matrix products  45 us (8%)
  other arithmetic  36.6 us (6%)
  between operations  14.6 us (2%)
  local copies, waits for them, and re-layouts  9.72 us (2%)
    psum x1, waiting for transfers between devices, on_device(): grad_up, grad_down = lax.psum((grad_up, grad_down), ('dp', 'seq'))  111 us
    pallas_call x4, Pallas kernels, swap_seq(): pl.pallas_call(swap_kernel, out_shape=jax.ShapeDtypeStruct(blocks.shape,...  108 us
    pallas_call x3, Pallas kernels, gather_rows(): pl.pallas_call(gather_kernel, out_shape=jax.ShapeDtypeStruct((4,) + block...  64.4 us
    pallas_call x3, Pallas kernels, scatter_sum(): pl.pallas_call(scatter_kernel, out_shape=jax.ShapeDtypeStruct(shape, F32)...  58.7 us
    psum x1, blocking collectives, on_device(): lax.psum(jnp.concatenate([vectors.reshape(-1), placed.reshape(-1)]), ('dp...  48.4 us
    dot_general x11, matrix products, dot(): return jnp.einsum(spec, a, b, preferred_element_type=F32)  45 us
    reduce_scatter x1, waiting for transfers between devices, on_device(): lax.psum_scatter(dot('cfe,ed->cfd', active, w_down).astype(BF16), 'tensor...  32.2 us
    pallas_call x1, Pallas kernels, attend_backward(): pl.pallas_call(functools.partial(attend_back_kernel, real), grid=(heads,)...  26.8 us
  transfers between devices with their start and end apart: 4, of which 3 were waited for; matrix products, arithmetic and copies ran while one was open for 8% of the time, Pallas kernels for 28%

profile of v1, /device:TPU:0, one launch (start us, length us, event | category | flops | bytes accessed | tf_op | source)
XLA Modules:
  0.0 582.0 jit_solution(5347563643825647366)
XLA Ops:
  12.1 25.2 %gather_rows.3.rows_ref = bf16[4,384,768]{2,1,0:T(8,128)(2,1)} custom-call(bf16[384,768]{1,0:T(8,128)(2,1)} %fusion.15.x_ref), custom_call_target="tpu_custom_call" | custom-call | tf_op jit(solution)/shard_map/gather_rows/pallas_call | solution.py:77
  38.3 5.4 project.1.x_ref
  43.7 34.7 %swap_seq.4 = bf16[4,576,384]{2,1,0:T(8,128)(2,1)} custom-call(bf16[4,576,384]{2,1,0:T(8,128)(2,1)} %project.1.x_ref), custom_call_target="tpu_custom_call" | custom-call | tf_op jit(solution)/shard_map/swap_seq/pallas_call | solution.py:164
  78.4 18.7 %attend_forward.1 = (bf16[4,3,64,384]{3,2,1,0:T(8,128)(2,1)}, f32[4,3,1,384]{3,2,1,0:T(1,128)}) custom-call(bf16[4,9,64,384]{3,2,1,0:T(8,128)(2,1)} %bitcast.79, bf16[4,9,64,384]{3,2,1,0:T(8,128)(2,1)} %bitcast.80, bf16[4,9,64,384]{3,2,1,0:T(8,128)(2,1)} %bitcast.81), custom_call_target="tpu_custom_call" | custom-call | tf_op jit(solution)/shard_map/attend_forward/pallas_call | solution.py:218
  97.1 22.7 %swap_seq.5 = bf16[4,192,384]{2,1,0:T(8,128)(2,1)} custom-call(bf16[4,192,384]{2,1,0:T(8,128)(2,1)} %bitcast.100), custom_call_target="tpu_custom_call" | custom-call | tf_op jit(solution)/shard_map/swap_seq/pallas_call | solution.py:164
  119.8 3.3 convolution_convert_fusion.3.x_ref
  123.2 20.0 %scatter_sum.3 = f32[384,768]{1,0:T(8,128)} custom-call(bf16[4,384,768]{2,1,0:T(8,128)(2,1)} %convolution_convert_fusion.3.x_ref), custom_call_target="tpu_custom_call" | custom-call | tf_op jit(solution)/shard_map/scatter_sum/pallas_call | solution.py:127
  146.1 19.9 %gather_rows.4 = bf16[4,384,768]{2,1,0:T(8,128)(2,1)} custom-call(bf16[384,768]{1,0:T(8,128)(2,1)} %add_convert_fusion.1.x_ref), custom_call_target="tpu_custom_call" | custom-call | tf_op jit(solution)/shard_map/gather_rows/pallas_call | solution.py:77
  166.0 4.9 fusion.26
  170.9 2.2 copy-done.9
  173.1 12.1 %multiply_convert_fusion = (bf16[4,384,768]{2,1,0:T(8,128)(2,1)}, f32[4,384,768]{2,1,0:T(8,128)}) fusion(f32[4,384,768]{2,1,0:T(8,128)S(1)} %get-tuple-element.65, f32[768]{0:T(1024)S(1)} %convert_element_type.124, u8[384,768]{1,0:T(8,128)(4,1)S(1)} %get-tuple-element.31, u8[384,768]{1,0:T(8,128)(4,1)S(1)} %get-tuple-element.30), kind=kLoop, calls=%fused_computation.9 | loop fusion | flops 83755008 | bytes 12389376 | tf_op jit(solution)/shard_map/convert_element_type | solution.py:360
  185.2 8.2 %convert_reduce_fusion = (f32[768]{0:T(1024)S(1)}, bf16[4,384,768]{2,1,0:T(8,128)(2,1)S(1)}) fusion(f32[4,384,768]{2,1,0:T(8,128)} %get-tuple-element.49, bf16[4,384,768]{2,1,0:T(8,128)(2,1)} %bitcast.111, bf16[768,768]{1,0:T(8,128)(2,1)} %param.25, f32[4,384,768]{2,1,0:T(8,128)} %copy-done.9, f32[768]{0:T(1024)S(1)} %convert_element_type.124), kind=kOutput, calls=%fused_computation.7 | convolution fusion | flops 1831992576 | bytes 15341568 | tf_op jit(solution)/shard_map/cfd,ed->cfe/dot_general | solution.py:315
  193.4 3.5 convolution_convert_fusion.1.x_ref
  196.9 3.1 bitcast_convert_fusion.1
  200.0 3.1 bitcast_convert_fusion
  203.1 19.9 %scatter_sum.4 = f32[384,768]{1,0:T(8,128)} custom-call(bf16[4,384,768]{2,1,0:T(8,128)(2,1)} %convolution_convert_fusion.1.x_ref), custom_call_target="tpu_custom_call" | custom-call | tf_op jit(solution)/shard_map/scatter_sum/pallas_call | solution.py:127
  227.2 19.3 %gather_rows.5 = bf16[4,384,768]{2,1,0:T(8,128)(2,1)} custom-call(bf16[384,768]{1,0:T(8,128)(2,1)} %convert_element_type.136.x_ref), custom_call_target="tpu_custom_call" | custom-call | tf_op jit(solution)/shard_map/gather_rows/pallas_call | solution.py:77
  246.6 3.6 fusion.12.x_ref
  251.5 15.6 %swap_seq.6 = bf16[4,192,384]{2,1,0:T(8,128)(2,1)} custom-call(bf16[4,192,384]{2,1,0:T(8,128)(2,1)} %fusion.12.x_ref), custom_call_target="tpu_custom_call" | custom-call | tf_op jit(solution)/shard_map/swap_seq/pallas_call | solution.py:164
  267.1 26.8 %attend_backward.1 = (bf16[4,3,64,384]{3,2,1,0:T(8,128)(2,1)}, bf16[4,3,64,384]{3,2,1,0:T(8,128)(2,1)}, bf16[4,3,64,384]{3,2,1,0:T(8,128)(2,1)}) custom-call(bf16[4,9,64,384]{3,2,1,0:T(8,128)(2,1)} %bitcast.82, bf16[4,9,64,384]{3,2,1,0:T(8,128)(2,1)} %bitcast.83, bf16[4,9,64,384]{3,2,1,0:T(8,128)(2,1)} %bitcast.84, bf16[4,3,64,384]{3,2,1,0:T(8,128)(2,1)} %bitcast.91, ...), custom_call_target="tpu_custom_call" | custom-call | tf_op jit(solution)/shard_map/attend_backward/pallas_call | solution.py:262
  293.9 2.8 pad_maximum_fusion.x_ref
  296.7 34.6 %swap_seq.7 = bf16[4,576,384]{2,1,0:T(8,128)(2,1)} custom-call(bf16[4,576,384]{2,1,0:T(8,128)(2,1)} %pad_maximum_fusion.x_ref), custom_call_target="tpu_custom_call" | custom-call | tf_op jit(solution)/shard_map/swap_seq/pallas_call | solution.py:164
  331.4 4.0 bitcast_convert_fusion.2
  335.5 5.1 convolution_convert_fusion.2
  341.7 4.9 convolution_convert_fusion.x_ref
  346.7 18.9 %scatter_sum.5 = f32[384,768]{1,0:T(8,128)} custom-call(bf16[4,384,768]{2,1,0:T(8,128)(2,1)} %convolution_convert_fusion.x_ref), custom_call_target="tpu_custom_call" | custom-call | tf_op jit(solution)/shard_map/scatter_sum/pallas_call | solution.py:127
  367.6 48.4 %psum.35 = f32[9216]{0:T(1024)S(1)} all-reduce(f32[9216]{0:T(1024)S(1)} %pad_maximum_fusion.1), channel_id=1, replica_groups=mesh['dp'=2,'seq'=4,'tensor'=4] {'dp','seq','tensor'}, use_global_device_ids=true, to_apply=%region_17.18 | all-reduce | flops 9216 | bytes 73728 | tf_op jit(solution)/shard_map/psum | solution.py:413
  419.7 2.7 all-reduce.9.cloned.1.call-done
  422.4 2.6 convert_element_type.146
  425.8 32.2 %reduce-scatter.2.cloned.1.call-done = bf16[1,384,768]{2,1,0:T(8,128)(2,1)} async-done(((bf16[4,384,768]{2,1,0:T(8,128)(2,1)}), bf16[1,384,768]{2,1,0:T(8,128)(2,1)}) %reduce-scatter.2.cloned.1.call-update) | async-done | bytes 589840 | tf_op jit(solution)/shard_map/reduce_scatter | solution.py:365
  460.1 110.6 %all-reduce.7.cloned.1.call-done = (bf16[768,768]{1,0:T(8,128)(2,1)}, bf16[768,768]{1,0:T(8,128)(2,1)}) async-done(((bf16[768,768]{1,0:T(8,128)(2,1)}, bf16[768,768]{1,0:T(8,128)(2,1)}), (bf16[768,768]{1,0:T(8,128)(2,1)}, bf16[768,768]{1,0:T(8,128)(2,1)})) %all-reduce.7.cloned.1.call-update) | async-done | bytes 2359312 | tf_op jit(solution)/shard_map/psum | solution.py:375
  570.6 3.0 convert_element_type.149
  (125 shorter events, 25.5 us)
Async XLA Ops:
  7.2 158.8 %copy-start = (bf16[768,768]{1,0:T(8,128)(2,1)S(1)}, bf16[768,768]{1,0:T(8,128)(2,1)}, u32[]{:S(2)}) copy-start(bf16[768,768]{1,0:T(8,128)(2,1)} %param.23) | copy-start | bytes 3538948
  7.2 3.4 copy-start.2
  7.2 3.7 copy-start.20
  7.2 3.7 copy-start.21
  7.2 178.0 %all-gather.3.cloned.1.call-start = ((), (), s32[]{:S(2)}) async-start(), calls=%async_computation.2 | async-start | bytes 2949120 | tf_op jit(solution)/shard_map/all_gather | solution.py:358
  9.3 413.1 %all-reduce.9.cloned.1.call-start = ((), (), s32[]{:S(2)}) async-start(), calls=%async_computation.4 | async-start | bytes 2359296 | tf_op jit(solution)/shard_map/psum | solution.py:393
  10.6 26.7 %copy-start.19 = (bf16[2,192]{1,0:T(2,128)(2,1)S(1)}, bf16[2,192]{1,0:T(2,128)(2,1)}, u32[]{:S(2)}) copy-start(bf16[2,192]{1,0:T(2,128)(2,1)} %param.18) | copy-start | bytes 2308
  78.4 41.4 %copy-start.17 = (bf16[192,768]{1,0:T(8,128)(2,1)S(1)}, bf16[192,768]{1,0:T(8,128)(2,1)}, u32[]{:S(2)}) copy-start(bf16[192,768]{1,0:T(8,128)(2,1)} %param.19) | copy-start | bytes 884740
  123.2 20.0 %copy-start.22 = (bf16[768]{0:T(1024)(128)(2,1)S(1)}, bf16[768]{0:T(1024)(128)(2,1)}, u32[]{:S(2)}) copy-start(bf16[768]{0:T(1024)(128)(2,1)} %param.20) | copy-start | bytes 4612
  143.1 1.8 copy-start.23
  143.2 1.8 copy-start.24
  145.0 21.0 %copy-start.25 = (bf16[768]{0:T(1024)(128)(2,1)S(1)}, bf16[768]{0:T(1024)(128)(2,1)}, u32[]{:S(2)}) copy-start(bf16[768]{0:T(1024)(128)(2,1)} %param.24) | copy-start | bytes 4612
  170.9 2.2 copy-start.9
  193.4 3.5 copy-start.11
  196.9 3.1 copy-start.13
  196.9 3.1 copy-start.27
  223.0 1.9 copy-start.4
  224.9 1.1 copy-start.14
  226.3 20.3 %copy-start.5 = (f32[384,768]{1,0:T(8,128)}, f32[384,768]{1,0:T(8,128)S(1)}, u32[]{:S(2)}) copy-start(f32[384,768]{1,0:T(8,128)S(1)} %get-tuple-element.43) | copy-start | bytes 3538948
  246.6 3.6 copy-start.10
  246.6 3.6 copy-start.12
  296.7 34.6 %copy-start.7 = (bf16[4,384,768]{2,1,0:T(8,128)(2,1)S(1)}, bf16[4,384,768]{2,1,0:T(8,128)(2,1)}, u32[]{:S(2)}) copy-start(bf16[4,384,768]{2,1,0:T(8,128)(2,1)} %gather_rows.3.rows_ref) | copy-start | bytes 7077892
  331.3 4.1 copy-start.28
  335.4 122.6 %reduce-scatter.2.cloned.1.call-start = ((), (), s32[]{:S(2)}) async-start(), calls=%async_computation.1 | async-start | bytes 2949120 | tf_op jit(solution)/shard_map/reduce_scatter | solution.py:365
  340.6 1.2 copy-start.16
  340.6 230.0 %all-reduce.7.cloned.1.call-start = ((), (), s32[]{:S(2)}) async-start(), calls=%async_computation.3 | async-start | bytes 4718592 | tf_op jit(solution)/shard_map/psum | solution.py:375
  346.7 18.9 %copy-start.8 = (bf16[4,576,384]{2,1,0:T(8,128)(2,1)S(1)}, bf16[4,576,384]{2,1,0:T(8,128)(2,1)}, u32[]{:S(2)}) copy-start(bf16[4,576,384]{2,1,0:T(8,128)(2,1)} %swap_seq.7) | copy-start | bytes 5308420
  365.5 1.3 copy-start.3
  416.8 1.9 copy-start.6
  422.4 2.6 copy-start.18
  570.6 3.0 copy-start.15
  570.6 4.6 copy-start.1
  (1 other events, 0.7 us)
Sparse Core Ops, SparseCore 0:
  10.2 33.1 all-gather.2
  335.5 86.8 all-reduce.8
  425.7 32.3 reduce-scatter.1
  461.5 109.0 all-reduce.6

commit v2 on v1

--- a/solution.py
+++ b/solution.py
@@ -143,6 +143,172 @@
         ),
         name="scatter_sum",
     )(blocks)
+
+
+def scatter_both_kernel(
+    x_ref, g_ref, o_ref, part_ref, got_far, got_own, mixed, got_sum, got_part,
+    a_send, a_recv, b_send, b_recv, c_send, c_recv, p_send, p_recv
+):
+    me, near, far, corner = tensor_peers()
+    here = lax.axis_index("seq")
+    ring = [lax.rem(here + hop, 4) for hop in (2, 1, 3)]
+    step = x_ref.shape[1] // PIECES
+    barrier = pltpu.get_barrier_semaphore()
+    for peer in (near, far):
+        pl.semaphore_signal(barrier, inc=1, device_id={"tensor": peer}, device_id_type=MESH)
+    for peer in ring:
+        pl.semaphore_signal(barrier, inc=1, device_id={"seq": peer}, device_id_type=MESH)
+    pl.semaphore_wait(barrier, 5)
+    spans = [pl.ds(piece * step, step) for piece in range(PIECES)]
+    first = [
+        remote("tensor", x_ref.at[corner, span], got_far.at[span], a_send.at[i], a_recv.at[i], near)
+        for i, span in enumerate(spans)
+    ]
+    second = remote("tensor", x_ref.at[near], got_own, b_send, b_recv, near)
+    across = [
+        remote("seq", g_ref.at[peer], got_part.at[i], p_send.at[i], p_recv.at[i], peer)
+        for i, peer in enumerate(ring)
+    ]
+    third = []
+    for i, span in enumerate(spans):
+        first[i].wait_recv()
+        mixed[span] = (x_ref[far, span].astype(F32) + got_far[span].astype(F32)).astype(BF16)
+        third.append(remote("tensor", mixed.at[span], got_sum.at[span], c_send.at[i], c_recv.at[i], far))
+    second.wait_recv()
+    for i, span in enumerate(spans):
+        third[i].wait_recv()
+        o_ref[span] = x_ref[me, span].astype(F32) + got_own[span].astype(F32) + got_sum[span].astype(F32)
+    total = g_ref[here].astype(F32)
+    for i in range(3):
+        across[i].wait_recv()
+        total = total + got_part[i].astype(F32)
+    part_ref[...] = total.astype(BF16)
+    second.wait_send()
+    for i in range(PIECES):
+        first[i].wait_send()
+        third[i].wait_send()
+    for copy in across:
+        copy.wait_send()
+
+
+def scatter_both(blocks, grads):
+    shape = blocks.shape[1:]
+    return pl.pallas_call(
+        scatter_both_kernel,
+        out_shape=(jax.ShapeDtypeStruct(shape, F32), jax.ShapeDtypeStruct(grads.shape[1:], BF16)),
+        in_specs=[pl.BlockSpec(memory_space=pltpu.VMEM)] * 2,
+        out_specs=(pl.BlockSpec(memory_space=pltpu.VMEM),) * 2,
+        scratch_shapes=[pltpu.VMEM(shape, BF16)] * 4
+        + [pltpu.VMEM((3,) + grads.shape[1:], BF16)]
+        + [
+            pltpu.SemaphoreType.DMA((PIECES,)),
+            pltpu.SemaphoreType.DMA((PIECES,)),
+            pltpu.SemaphoreType.DMA,
+            pltpu.SemaphoreType.DMA,
+            pltpu.SemaphoreType.DMA((PIECES,)),
+            pltpu.SemaphoreType.DMA((PIECES,)),
+            pltpu.SemaphoreType.DMA((3,)),
+            pltpu.SemaphoreType.DMA((3,)),
+        ],
+        compiler_params=pltpu.CompilerParams(
+            collective_id=4, has_side_effects=True, vmem_limit_bytes=VMEM_BYTES
+        ),
+        name="scatter_both",
+    )(blocks, grads)
+
+
+def finish_kernel(
+    dp_size, part_ref, vec_ref, local_ref, o_ref, vec_out,
+    full, got_dp, got_vec, vec_sum, seq_vec, dp_vec, dp_mix,
+    d_send, d_recv, a_send, a_recv, s_send, s_recv, e_send, e_recv, g_send, g_recv
+):
+    tensor_at, here, group = lax.axis_index("tensor"), lax.axis_index("seq"), lax.axis_index("dp")
+    columns = [lax.rem(tensor_at + hop, 4) for hop in (1, 2, 3)]
+    ring = [lax.rem(here + hop, 4) for hop in (2, 1, 3)]
+    others = [lax.rem(group + hop, dp_size) for hop in range(1, dp_size)]
+    barrier = pltpu.get_barrier_semaphore()
+    for axis, peers in (("tensor", columns), ("seq", ring), ("dp", others)):
+        for peer in peers:
+            pl.semaphore_signal(barrier, inc=1, device_id={axis: peer}, device_id_type=MESH)
+    pl.semaphore_wait(barrier, 6 + len(others))
+    parts = [
+        remote("dp", part_ref, got_dp.at[group], d_send.at[i], d_recv.at[i], peer) for i, peer in enumerate(others)
+    ]
+    vectors = [
+        remote("tensor", vec_ref.at[peer], got_vec.at[i], a_send.at[i], a_recv.at[i], peer)
+        for i, peer in enumerate(columns)
+    ]
+    got_dp[group] = part_ref[...]
+    total = vec_ref[tensor_at]
+    for i in range(3):
+        vectors[i].wait_recv()
+        total = total + got_vec[i]
+    vec_sum[0:8] = total
+    vec_sum[8:16] = local_ref[...]
+    seq_vec[here] = vec_sum[...]
+    around = [
+        remote("seq", vec_sum, seq_vec.at[here], s_send.at[i], s_recv.at[i], peer) for i, peer in enumerate(ring)
+    ]
+    for copy in parts:
+        copy.wait_recv()
+    total = got_dp[0].astype(F32)
+    for i in range(1, dp_size):
+        total = total + got_dp[i].astype(F32)
+    full[here] = total.astype(BF16)
+    spread = [
+        remote("seq", full.at[here], full.at[here], g_send.at[i], g_recv.at[i], peer) for i, peer in enumerate(ring)
+    ]
+    for copy in around:
+        copy.wait_recv()
+    dp_mix[...] = seq_vec[0] + seq_vec[1] + seq_vec[2] + seq_vec[3]
+    dp_vec[group] = dp_mix[...]
+    last = [
+        remote("dp", dp_mix, dp_vec.at[group], e_send.at[i], e_recv.at[i], peer) for i, peer in enumerate(others)
+    ]
+    for copy in last:
+        copy.wait_recv()
+    total = dp_vec[0]
+    for i in range(1, dp_size):
+        total = total + dp_vec[i]
+    vec_out[...] = total
+    for copy in spread:
+        copy.wait_recv()
+    for i in range(4):
+        o_ref[i] = full[i].astype(F32)
+    for copy in parts + vectors + around + spread + last:
+        copy.wait_send()
+
+
+def finish(part, vectors, local, dp_size):
+    rows, depth = part.shape
+    vec = local.shape
+    wide = (2 * vec[0], vec[1])
+    vmem = pl.BlockSpec(memory_space=pltpu.VMEM)
+    pair = lambda n: [pltpu.SemaphoreType.DMA((n,)), pltpu.SemaphoreType.DMA((n,))]
+    return pl.pallas_call(
+        functools.partial(finish_kernel, dp_size),
+        out_shape=(jax.ShapeDtypeStruct((4, rows, depth), F32), jax.ShapeDtypeStruct(wide, F32)),
+        in_specs=[vmem] * 3,
+        out_specs=(vmem, vmem),
+        scratch_shapes=[
+            pltpu.VMEM((4, rows, depth), BF16),
+            pltpu.VMEM((dp_size, rows, depth), BF16),
+            pltpu.VMEM((3,) + vec, F32),
+            pltpu.VMEM(wide, F32),
+            pltpu.VMEM((4,) + wide, F32),
+            pltpu.VMEM((dp_size,) + wide, F32),
+            pltpu.VMEM(wide, F32),
+        ]
+        + pair(dp_size - 1)
+        + pair(3)
+        + pair(3)
+        + pair(dp_size - 1)
+        + pair(3),
+        compiler_params=pltpu.CompilerParams(
+            collective_id=5, has_side_effects=True, vmem_limit_bytes=VMEM_BYTES
+        ),
+        name="finish",
+    )(part, vectors, local)
 
 
 def swap_kernel(x_ref, o_ref, own_sem, send, recv):
@@ -364,15 +530,13 @@
     grad_norm_two = dot("cfe,de->cfd", grad_pre, w_up).astype(BF16)
     branch_two = lax.psum_scatter(
         dot("cfe,ed->cfd", active, w_down).astype(BF16), "tensor", scatter_dimension=0, tiled=False
-    ).astype(F32)
-    output = (hidden + branch_two + b_down.astype(F32)).astype(BF16)
+    )
     grad_down = dot("cfe,cfd->ed", active, cot_rows)
     grad_up_bias = jnp.sum(grad_pre, axis=(0, 1), dtype=F32)
     grad_up = dot("cfd,cfe->de", rows_two, grad_pre)
     grad_up, grad_down, grad_norm_two = lax.optimization_barrier(
         (grad_up.astype(BF16), grad_down.astype(BF16), grad_norm_two)
     )
-    grad_up, grad_down = lax.psum((grad_up, grad_down), ("dp", "seq"))
     grad_norm_two = scatter_sum(grad_norm_two)
 
     _, pull_two = jax.vjp(layer_norm, hidden, gain_two, shift_two)
@@ -381,17 +545,22 @@
     hidden_low = grad_hidden.astype(BF16)
     grad_rows = gather_rows(hidden_low)
     grad_att = dot("cfd,ed->cef", grad_rows, w_out).astype(BF16)
-    grad_out = dot("cef,cfd->ed", attended, grad_rows)
+    grad_out = dot("cef,cfd->ed", attended, grad_rows).astype(BF16)
+    grad_up, grad_down, grad_out, grad_att = lax.optimization_barrier((grad_up, grad_down, grad_out, grad_att))
+    grad_up, grad_down, grad_out = lax.psum((grad_up, grad_down, grad_out), ("dp", "seq"))
     grad_att = swap_seq(grad_att, 3).reshape(clips, heads, HEAD_DIM, span)
     grads = attend_backward(qkv, grad_att, lse, heads, real)
     grad_qkv_cols = jnp.concatenate([g.reshape(clips, width, span) for g in grads], axis=1)
     grad_qkv_cols = swap_seq(grad_qkv_cols, 2)
-    grad_norm_one = scatter_sum(dot("ckf,kd->cfd", grad_qkv_cols, w_flat).astype(BF16))
+    grad_norm_one = dot("ckf,kd->cfd", grad_qkv_cols, w_flat).astype(BF16)
     bias_sums = jnp.sum(grad_qkv_cols, axis=(0, 2), dtype=F32).reshape(3, width)
-    grad_qkv = dot("cfd,ckf->dk", rows_one, grad_qkv_cols)
-    grad_qkv, grad_out = grad_qkv.astype(BF16), grad_out.astype(BF16)
-    grad_qkv, grad_out = lax.psum((grad_qkv, grad_out), ("seq", "dp"))
-    grad_qkv = jnp.swapaxes(grad_qkv.reshape(depth, 3, width), 0, 1).astype(F32)
+    grad_qkv = dot("ckf,cfd->kd", grad_qkv_cols, rows_one).astype(BF16)
+    grad_up, grad_down, grad_out, branch_two, grad_norm_one = lax.optimization_barrier(
+        (grad_up, grad_down, grad_out, branch_two, grad_norm_one)
+    )
+    output = (hidden + branch_two.astype(F32) + b_down.astype(F32)).astype(BF16)
+    seq_size = lax.axis_size("seq")
+    grad_norm_one, grad_part = scatter_both(grad_norm_one, grad_qkv.reshape(seq_size, -1, depth))
 
     _, pull_one = jax.vjp(layer_norm, resid, gain_one, shift_one)
     grad_resid, grad_gain_one, grad_shift_one = pull_one(grad_norm_one)
@@ -406,28 +575,31 @@
             jnp.sum(cot.astype(F32), axis=0),
         ]
     )
-    me = lax.axis_index("tensor")
-    parts = lax.axis_size("tensor")
-    local = jnp.concatenate([bias_sums[0], bias_sums[2], grad_up_bias])
-    placed = jnp.where(jnp.arange(parts)[:, None] == me, local[None], 0.0)
-    flat = lax.psum(jnp.concatenate([vectors.reshape(-1), placed.reshape(-1)]), ("dp", "seq", "tensor"))
-    vectors = lax.dynamic_slice_in_dim(flat[: vectors.size].reshape(vectors.shape), me * width, width, 1)
-    local = lax.dynamic_slice_in_dim(flat[vectors.shape[0] * depth :].reshape(parts, -1), me, 1, 0)[0]
+    parts = depth // width
+    lanes = -(-width // 128) * 128
+    vectors = jnp.swapaxes(vectors.reshape(6, parts, width), 0, 1)
+    vectors = jnp.pad(vectors, ((0, 0), (0, 2), (0, lanes - width)))
+    hidden_parts = grad_up_bias.reshape(-1, width)
+    local = jnp.concatenate([bias_sums[0][None], bias_sums[2][None], hidden_parts])
+    local = jnp.pad(local, ((0, 8 - local.shape[0]), (0, lanes - width)))
+    grad_qkv, small = finish(grad_part, vectors, local, lax.axis_size("dp"))
+    grad_qkv = jnp.swapaxes(grad_qkv.reshape(3, width, depth), 1, 2)
+    small = small[:, :width]
     return (
         output[None, :real],
         grad_tokens[None, :real],
-        vectors[0],
-        vectors[1],
+        small[0],
+        small[1],
         grad_qkv,
-        local[: 2 * width].reshape(2, width),
+        small[8:10],
         grad_out.astype(F32),
-        vectors[2],
-        vectors[3],
-        vectors[4],
+        small[2],
+        small[3],
+        small[4],
         grad_up.astype(F32),
-        local[2 * width :],
+        small[10 : 10 + hidden_parts.shape[0]].reshape(-1),
         grad_down.astype(F32),
-        vectors[5],
+        small[5],
     )
 
 

time: 592 us -> 499 us (0.84)
  waiting for transfers between devices: 146 us -> 38.4 us
  Pallas kernels: 282 us -> 341 us
  blocking collectives: 48.4 us -> 0 us
  other arithmetic: 36.6 us -> 44.6 us
    psum x2 -> x1, waiting for transfers between devices: 113 us -> 38.3 us  [on_device(): lax.psum((grad_up, grad_down, grad_out), ('dp', 'seq'))]
    pallas_call x0 -> x2, Pallas kernels: none -> 51.9 us  [the longest x1 30.9 us: finish(): pl.pallas_call(functools.partial(finish_kernel, dp_size), out_shape=(jax....]
    psum x1 -> x0, blocking collectives: 48.4 us -> none  [on_device(): lax.psum(jnp.concatenate([vectors.reshape(-1), placed.reshape(-1)]), ('dp...]
    reduce_scatter x1, waiting for transfers between devices: 32.2 us -> 0.01 us  [on_device(): lax.psum_scatter(dot('cfe,ed->cfd', active, w_down).astype(BF16), 'tensor...]
    pallas_call x4, Pallas kernels: 108 us -> 124 us  [swap_seq(): pl.pallas_call(swap_kernel, out_shape=jax.ShapeDtypeStruct(blocks.shape,...]
    convert_element_type x1, other arithmetic: 12.1 us -> 22.5 us  [on_device(): active = gelu_exact(pre_act).astype(BF16)]
    pallas_call x3 -> x2, Pallas kernels: 58.7 us -> 48.8 us  [scatter_sum(): pl.pallas_call(scatter_kernel, out_shape=jax.ShapeDtypeStruct(shape, F32)...]
  transfers between devices with their start and end apart: 4 -> 3, of which waited for: 3 -> 1; matrix products, arithmetic and copies ran while one was open for 8% -> 16% of each run, Pallas kernels for 28% -> 59%
where the time goes in v2:
time: 499 us; the launch traced here: 493 us
  Pallas kernels  341 us (68%)
  other arithmetic  44.6 us (9%)
  matrix products  42 us (8%)
  waiting for transfers between devices  38.4 us (8%)
  between operations  14.7 us (3%)
  local copies, waits for them, and re-layouts  12.9 us (3%)
    pallas_call x4, Pallas kernels, swap_seq(): pl.pallas_call(swap_kernel, out_shape=jax.ShapeDtypeStruct(blocks.shape,...  124 us
    pallas_call x3, Pallas kernels, gather_rows(): pl.pallas_call(gather_kernel, out_shape=jax.ShapeDtypeStruct((4,) + block...  64.4 us
    pallas_call x2, Pallas kernels, scatter_sum(): pl.pallas_call(scatter_kernel, out_shape=jax.ShapeDtypeStruct(shape, F32)...  48.8 us
    dot_general x11, matrix products, dot(): return jnp.einsum(spec, a, b, preferred_element_type=F32)  42 us
    psum x1, waiting for transfers between devices, on_device(): lax.psum((grad_up, grad_down, grad_out), ('dp', 'seq'))  38.3 us
    pallas_call x1, Pallas kernels, finish(): pl.pallas_call(functools.partial(finish_kernel, dp_size), out_shape=(jax....  30.9 us
    pallas_call x1, Pallas kernels, attend_backward(): pl.pallas_call(functools.partial(attend_back_kernel, real), grid=(heads,)...  27 us
    convert_element_type x1, other arithmetic, on_device(): active = gelu_exact(pre_act).astype(BF16)  22.5 us
  transfers between devices with their start and end apart: 3, of which 1 were waited for; matrix products, arithmetic and copies ran while one was open for 16% of the time, Pallas kernels for 59%

profile of v2, /device:TPU:0, one launch (start us, length us, event | category | flops | bytes accessed | tf_op | source)
XLA Modules:
  0.0 493.4 jit_solution(792149674753018558)
XLA Ops:
  7.3 2.0 pad.16
  12.1 25.2 %gather_rows.3.rows_ref = bf16[4,384,768]{2,1,0:T(8,128)(2,1)} custom-call(bf16[384,768]{1,0:T(8,128)(2,1)} %fusion.15.x_ref), custom_call_target="tpu_custom_call" | custom-call | tf_op jit(solution)/shard_map/gather_rows/pallas_call | solution.py:77
  38.3 5.4 %project.1.x_ref = bf16[4,576,384]{2,1,0:T(8,128)(2,1)} custom-call(bf16[4,384,768]{2,1,0:T(8,128)(2,1)} %gather_rows.3.rows_ref, bf16[576,768]{1,0:T(8,128)(2,1)} %bitcast.99, f32[576,1]{1,0:T(8,128)} %broadcast_in_dim.24.b_ref), custom_call_target="tpu_custom_call" | custom-call | tf_op jit(solution)/shard_map/project/pallas_call | solution.py:455
  43.7 34.7 %swap_seq.4 = bf16[4,576,384]{2,1,0:T(8,128)(2,1)} custom-call(bf16[4,576,384]{2,1,0:T(8,128)(2,1)} %project.1.x_ref), custom_call_target="tpu_custom_call" | custom-call | tf_op jit(solution)/shard_map/swap_seq/pallas_call | solution.py:330
  78.4 18.7 %attend_forward.1 = (bf16[4,3,64,384]{3,2,1,0:T(8,128)(2,1)}, f32[4,3,1,384]{3,2,1,0:T(1,128)}) custom-call(bf16[4,9,64,384]{3,2,1,0:T(8,128)(2,1)} %bitcast.82, bf16[4,9,64,384]{3,2,1,0:T(8,128)(2,1)} %bitcast.83, bf16[4,9,64,384]{3,2,1,0:T(8,128)(2,1)} %bitcast.84), custom_call_target="tpu_custom_call" | custom-call | tf_op jit(solution)/shard_map/attend_forward/pallas_call | solution.py:384
  97.1 22.7 %swap_seq.5 = bf16[4,192,384]{2,1,0:T(8,128)(2,1)} custom-call(bf16[4,192,384]{2,1,0:T(8,128)(2,1)} %bitcast.104), custom_call_target="tpu_custom_call" | custom-call | tf_op jit(solution)/shard_map/swap_seq/pallas_call | solution.py:330
  119.8 3.3 convolution_convert_fusion.3.x_ref
  123.1 20.0 %scatter_sum.2 = f32[384,768]{1,0:T(8,128)} custom-call(bf16[4,384,768]{2,1,0:T(8,128)(2,1)} %convolution_convert_fusion.3.x_ref), custom_call_target="tpu_custom_call" | custom-call | tf_op jit(solution)/shard_map/scatter_sum/pallas_call | solution.py:127
  146.1 19.9 %gather_rows.4 = bf16[4,384,768]{2,1,0:T(8,128)(2,1)} custom-call(bf16[384,768]{1,0:T(8,128)(2,1)} %add_convert_fusion.1.x_ref), custom_call_target="tpu_custom_call" | custom-call | tf_op jit(solution)/shard_map/gather_rows/pallas_call | solution.py:77
  166.0 4.9 fusion.26
  170.9 22.5 %multiply_convert_fusion = (bf16[4,384,768]{2,1,0:T(8,128)(2,1)S(1)}, f32[4,384,768]{2,1,0:T(8,128)}) fusion(f32[4,384,768]{2,1,0:T(8,128)S(1)} %get-tuple-element.88, f32[768]{0:T(1024)S(1)} %convert_element_type.117, u8[384,768]{1,0:T(8,128)(4,1)S(1)} %get-tuple-element.57, u8[384,768]{1,0:T(8,128)(4,1)S(1)} %get-tuple-element.56), kind=kLoop, calls=%fused_computation.8 | loop fusion | flops 83755008 | bytes 12389376 | tf_op jit(solution)/shard_map/convert_element_type | solution.py:526
  194.8 3.4 convolution_convert_fusion.1
  198.4 8.2 %convert_reduce_fusion = (f32[768]{0:T(1024)S(1)}, bf16[4,384,768]{2,1,0:T(8,128)(2,1)S(1)}) fusion(f32[4,384,768]{2,1,0:T(8,128)} %get-tuple-element.74, bf16[4,384,768]{2,1,0:T(8,128)(2,1)} %bitcast.118, bf16[768,768]{1,0:T(8,128)(2,1)} %param.25, f32[4,384,768]{2,1,0:T(8,128)} %copy-done.8, f32[768]{0:T(1024)S(1)} %convert_element_type.117), kind=kOutput, calls=%fused_computation.7 | convolution fusion | flops 1831992576 | bytes 15341568 | tf_op jit(solution)/shard_map/cfd,ed->cfe/dot_general | solution.py:481
  206.6 3.5 convolution_convert_fusion.2.x_ref
  210.0 3.1 bitcast_convert_fusion.1
  213.2 3.1 bitcast_convert_fusion
  216.3 28.9 %scatter_sum.3 = f32[384,768]{1,0:T(8,128)} custom-call(bf16[4,384,768]{2,1,0:T(8,128)(2,1)} %convolution_convert_fusion.2.x_ref), custom_call_target="tpu_custom_call" | custom-call | tf_op jit(solution)/shard_map/scatter_sum/pallas_call | solution.py:127
  245.2 1.9 multiply_reduce_fusion
  249.4 19.3 %gather_rows.5 = bf16[4,384,768]{2,1,0:T(8,128)(2,1)} custom-call(bf16[384,768]{1,0:T(8,128)(2,1)} %convert_element_type.124.x_ref), custom_call_target="tpu_custom_call" | custom-call | tf_op jit(solution)/shard_map/gather_rows/pallas_call | solution.py:77
  268.7 3.6 fusion.12.x_ref
  273.6 21.9 %swap_seq.6 = bf16[4,192,384]{2,1,0:T(8,128)(2,1)} custom-call(bf16[4,192,384]{2,1,0:T(8,128)(2,1)} %fusion.12.x_ref), custom_call_target="tpu_custom_call" | custom-call | tf_op jit(solution)/shard_map/swap_seq/pallas_call | solution.py:330
  295.5 27.0 %attend_backward.1 = (bf16[4,3,64,384]{3,2,1,0:T(8,128)(2,1)}, bf16[4,3,64,384]{3,2,1,0:T(8,128)(2,1)}, bf16[4,3,64,384]{3,2,1,0:T(8,128)(2,1)}) custom-call(bf16[4,9,64,384]{3,2,1,0:T(8,128)(2,1)} %bitcast.85, bf16[4,9,64,384]{3,2,1,0:T(8,128)(2,1)} %bitcast.86, bf16[4,9,64,384]{3,2,1,0:T(8,128)(2,1)} %bitcast.87, bf16[4,3,64,384]{3,2,1,0:T(8,128)(2,1)} %bitcast.94, ...), custom_call_target="tpu_custom_call" | custom-call | tf_op jit(solution)/shard_map/attend_backward/pallas_call | solution.py:428
  322.5 2.8 pad_maximum_fusion.x_ref
  325.4 45.1 %swap_seq.7 = bf16[4,576,384]{2,1,0:T(8,128)(2,1)} custom-call(bf16[4,576,384]{2,1,0:T(8,128)(2,1)} %pad_maximum_fusion.x_ref), custom_call_target="tpu_custom_call" | custom-call | tf_op jit(solution)/shard_map/swap_seq/pallas_call | solution.py:330
  370.9 1.8 convert_reduce_fusion.1
  373.3 5.1 %convolution_convert_fusion.x_ref = bf16[4,384,768]{2,1,0:T(8,128)(2,1)} fusion(bf16[4,576,384]{2,1,0:T(8,128)(2,1)} %swap_seq.7, bf16[576,768,1]{1,0,2:T(8,128)(2,1)S(1)} %bitcast.100), kind=kOutput, calls=%fused_computation.25 | convolution fusion | flops 1360134144 | bytes 5013504 | tf_op jit(solution)/shard_map/ckf,kd->cfd/dot_general | solution.py:481
  378.4 2.5 bitcast_convert_fusion.2
  380.8 38.3 %all-reduce.7.cloned.1.call-done = (bf16[768,768]{1,0:T(8,128)(2,1)}, bf16[768,768]{1,0:T(8,128)(2,1)}, bf16[192,768]{1,0:T(8,128)(2,1)}) async-done(((bf16[768,768]{1,0:T(8,128)(2,1)}, bf16[768,768]{1,0:T(8,128)(2,1)}, bf16[192,768]{1,0:T(8,128)(2,1)}), (bf16[768,768]{1,0:T(8,128)(2,1)}, bf16[768,768]{1,0:T(8,128)(2,1)}, bf16[192,768]{1,0:T(8,128)(2,1)})) %all-reduce.7.cloned.1.call-update) | async-done | bytes 2654224 | tf_op jit(solution)/shard_map/psum | solution.py:550
  419.1 21.1 %scatter_both.1 = (f32[384,768]{1,0:T(8,128)}, bf16[144,768]{1,0:T(8,128)(2,1)}) custom-call(bf16[4,384,768]{2,1,0:T(8,128)(2,1)} %convolution_convert_fusion.x_ref, bf16[4,144,768]{2,1,0:T(8,128)(2,1)} %bitcast.98), custom_call_target="tpu_custom_call" | custom-call | tf_op jit(solution)/shard_map/scatter_both/pallas_call | solution.py:196
  440.3 1.9 fusion.16
  443.0 30.9 %finish.1 = (f32[4,144,768]{2,1,0:T(8,128)}, f32[16,256]{1,0:T(8,128)}) custom-call(bf16[144,768]{1,0:T(8,128)(2,1)} %get-tuple-element.50.part_ref, f32[4,8,256]{2,1,0:T(8,128)} %pad.17.vec_ref, f32[8,256]{1,0:T(8,128)} %select_maximum_fusion.local_ref), custom_call_target="tpu_custom_call" | custom-call | tf_op jit(solution)/shard_map/finish/pallas_call | solution.py:288
  480.9 1.6 convert_element_type.139
  (123 shorter events, 24.6 us)
Async XLA Ops:
  7.2 158.8 %copy-start = (bf16[768,768]{1,0:T(8,128)(2,1)S(1)}, bf16[768,768]{1,0:T(8,128)(2,1)}, u32[]{:S(2)}) copy-start(bf16[768,768]{1,0:T(8,128)(2,1)} %param.23) | copy-start | bytes 3538948
  7.2 3.4 copy-start.2
  7.2 3.7 copy-start.24
  7.2 3.7 copy-start.25
  7.2 191.1 %all-gather.3.cloned.1.call-start = ((), (), s32[]{:S(2)}) async-start(), calls=%async_computation.2 | async-start | bytes 2949120 | tf_op jit(solution)/shard_map/all_gather | solution.py:524
  9.3 371.5 %reduce-scatter.2.cloned.1.call-start = ((), (), s32[]{:S(2)}) async-start(), calls=%async_computation.1 | async-start | bytes 2949120 | tf_op jit(solution)/shard_map/reduce_scatter | solution.py:531
  10.6 26.7 %copy-start.23 = (bf16[2,192]{1,0:T(2,128)(2,1)S(1)}, bf16[2,192]{1,0:T(2,128)(2,1)}, u32[]{:S(2)}) copy-start(bf16[2,192]{1,0:T(2,128)(2,1)} %param.18) | copy-start | bytes 2308
  78.4 41.4 %copy-start.21 = (bf16[192,768]{1,0:T(8,128)(2,1)S(1)}, bf16[192,768]{1,0:T(8,128)(2,1)}, u32[]{:S(2)}) copy-start(bf16[192,768]{1,0:T(8,128)(2,1)} %param.19) | copy-start | bytes 884740
  123.1 20.0 %copy-start.26 = (bf16[768]{0:T(1024)(128)(2,1)S(1)}, bf16[768]{0:T(1024)(128)(2,1)}, u32[]{:S(2)}) copy-start(bf16[768]{0:T(1024)(128)(2,1)} %param.20) | copy-start | bytes 4612
  143.1 1.8 copy-start.27
  143.1 1.8 copy-start.28
  145.0 21.0 %copy-start.29 = (bf16[768]{0:T(1024)(128)(2,1)S(1)}, bf16[768]{0:T(1024)(128)(2,1)}, u32[]{:S(2)}) copy-start(bf16[768]{0:T(1024)(128)(2,1)} %param.24) | copy-start | bytes 4612
  170.9 22.5 %copy-start.8 = (f32[4,384,768]{2,1,0:T(8,128)}, f32[4,384,768]{2,1,0:T(8,128)S(1)}, u32[]{:S(2)}) copy-start(f32[4,384,768]{2,1,0:T(8,128)S(1)} %get-tuple-element.88) | copy-start | bytes 14155780
  170.9 23.9 %copy-start.32 = (bf16[768,768]{1,0:T(8,128)(2,1)S(1)}, bf16[768,768]{1,0:T(8,128)(2,1)}, u32[]{:S(2)}) copy-start(bf16[768,768]{1,0:T(8,128)(2,1)} %param.25) | copy-start | bytes 3538948
  198.3 220.9 %all-reduce.7.cloned.1.call-start = ((), (), s32[]{:S(2)}) async-start(), calls=%async_computation.3 | async-start | bytes 5308416 | tf_op jit(solution)/shard_map/psum | solution.py:550
  206.6 3.5 copy-start.11
  210.0 3.2 copy-start.14
  210.0 3.2 copy-start.31
  245.2 1.9 copy-start.3
  248.4 20.3 %copy-start.4 = (f32[384,768]{1,0:T(8,128)}, f32[384,768]{1,0:T(8,128)S(1)}, u32[]{:S(2)}) copy-start(f32[384,768]{1,0:T(8,128)S(1)} %get-tuple-element.68) | copy-start | bytes 3538948
  268.6 3.6 copy-start.10
  268.7 3.6 copy-start.12
  325.3 47.9 %copy-start.19 = (bf16[3,768,192]{1,2,0:T(8,128)(2,1)S(1)}, bf16[3,768,192]{1,2,0:T(8,128)(2,1)}, u32[]{:S(2)}) copy-start(bf16[3,768,192]{1,2,0:T(8,128)(2,1)} %param.17) | copy-start | bytes 2654212
  373.3 5.1 %copy-start.6 = (bf16[4,384,768]{2,1,0:T(8,128)(2,1)S(1)}, bf16[4,384,768]{2,1,0:T(8,128)(2,1)}, u32[]{:S(2)}) copy-start(bf16[4,384,768]{2,1,0:T(8,128)(2,1)} %gather_rows.3.rows_ref) | copy-start | bytes 7077892
  373.3 5.1 %copy-start.7 = (bf16[4,576,384]{2,1,0:T(8,128)(2,1)S(1)}, bf16[4,576,384]{2,1,0:T(8,128)(2,1)}, u32[]{:S(2)}) copy-start(bf16[4,576,384]{2,1,0:T(8,128)(2,1)} %swap_seq.7) | copy-start | bytes 5308420
  440.2 37.8 %copy-start.9 = (f32[384,768]{1,0:T(8,128)S(1)}, f32[384,768]{1,0:T(8,128)}, u32[]{:S(2)}) copy-start(f32[384,768]{1,0:T(8,128)} %get-tuple-element.49) | copy-start | bytes 3538948
  478.6 2.3 copy-start.17
  480.9 1.6 copy-start.22
  480.9 2.4 copy-start.5
  480.9 2.4 copy-start.20
  483.3 1.9 copy-start.16
  483.3 3.1 copy-start.1
  (4 other events, 5.1 us)
Sparse Core Ops, SparseCore 0:
  10.2 33.1 all-gather.2
  198.4 42.9 reduce-scatter.1
  273.7 145.3 all-reduce.6

commit v3 on v2

--- a/solution.py
+++ b/solution.py
@@ -311,39 +311,6 @@
     )(part, vectors, local)
 
 
-def swap_kernel(x_ref, o_ref, own_sem, send, recv):
-    me = lax.axis_index("seq")
-    peers = [lax.rem(me + hop, 4) for hop in (2, 1, 3)]
-    greet("seq", peers)
-    copies = [
-        remote("seq", x_ref.at[peer], o_ref.at[me], send.at[i], recv.at[i], peer)
-        for i, peer in enumerate(peers)
-    ]
-    own = pltpu.make_async_copy(x_ref.at[me], o_ref.at[me], own_sem)
-    own.start()
-    own.wait()
-    for copy in copies:
-        copy.wait()
-
-
-def swap_seq(blocks, ident):
-    return pl.pallas_call(
-        swap_kernel,
-        out_shape=jax.ShapeDtypeStruct(blocks.shape, blocks.dtype),
-        in_specs=[pl.BlockSpec(memory_space=pl.ANY)],
-        out_specs=pl.BlockSpec(memory_space=pl.ANY),
-        scratch_shapes=[
-            pltpu.SemaphoreType.DMA,
-            pltpu.SemaphoreType.DMA((3,)),
-            pltpu.SemaphoreType.DMA((3,)),
-        ],
-        compiler_params=pltpu.CompilerParams(
-            collective_id=ident, has_side_effects=True, vmem_limit_bytes=VMEM_BYTES
-        ),
-        name="swap_seq",
-    )(blocks)
-
-
 def rows_dot(a, b):
     return lax.dot_general(a, b, (((0,), (0,)), ((), ())), preferred_element_type=F32)
 
@@ -352,8 +319,12 @@
     return lax.dot_general(a, b, (((1,), (1,)), ((), ())), preferred_element_type=F32)
 
 
-def side_by_side(ref):
-    return jnp.concatenate([ref[i, 0] for i in range(ref.shape[0])], axis=1)
+def seq_ring(me):
+    return [lax.rem(me + hop, 4) for hop in (2, 1, 3)]
+
+
+def head_cols(ref, head, first):
+    return jnp.concatenate([ref[i, head, first : first + HEAD_DIM] for i in range(ref.shape[0])], axis=1)
 
 
 def masked_scores(key_cols, query_cols, span, real):
@@ -362,94 +333,155 @@
     return jnp.where(lax.rem(row, span) < real, scores, -1e30)
 
 
-def attend_kernel(real, q_ref, k_ref, v_ref, o_ref, lse_ref):
-    shards, _, _, span = q_ref.shape
-    key_cols, value_cols = side_by_side(k_ref), side_by_side(v_ref)
-    for i in range(shards):
-        scores = masked_scores(key_cols, q_ref[i, 0], span, real)
-        top = jnp.max(scores, axis=0, keepdims=True)
-        expo = jnp.exp(scores - top)
-        total = jnp.sum(expo, axis=0, keepdims=True)
-        probs = (expo * (1.0 / total)).astype(BF16)
-        o_ref[i, 0] = jnp.dot(value_cols, probs, preferred_element_type=F32).astype(BF16)
-        lse_ref[i, 0] = top + jnp.log(total)
-
-
-def head_spec(shards, span, offset):
-    return pl.BlockSpec((shards, 1, HEAD_DIM, span), lambda h: (0, offset + h, 0, 0))
-
-
-def attend_forward(qkv, heads, real):
-    shards, _, _, span = qkv.shape
+def chunk(src, dst, send, recv, peer):
+    return pltpu.make_async_remote_copy(
+        src_ref=src, dst_ref=dst, send_sem=send, recv_sem=recv, device_id={"seq": peer}, device_id_type=MESH
+    )
+
+
+def attend_kernel(real, x_ref, qkv_ref, o_ref, lse_ref, got, att, back, x_send, x_recv, o_send, o_recv):
+    me = lax.axis_index("seq")
+    ring = seq_ring(me)
+    _, heads, _, span = x_ref.shape
+    greet("seq", ring)
+
+    def arrival(h, k):
+        return chunk(x_ref.at[ring[k], h], got.at[me, h], x_send.at[h, k], x_recv.at[h, k], ring[k])
+
+    def result(h, k):
+        return chunk(att.at[ring[k], h], back.at[me, h], o_send.at[h, k], o_recv.at[h, k], ring[k])
+
+    for h in range(heads):
+        for k in range(3):
+            arrival(h, k).start()
+    got[me] = x_ref[me]
+
+    def one_head(h, carry):
+        for k in range(3):
+            arrival(h, k).wait_recv()
+        key_cols, value_cols = head_cols(got, h, HEAD_DIM), head_cols(got, h, 2 * HEAD_DIM)
+        for k, i in enumerate(ring + [me]):
+            scores = masked_scores(key_cols, got[i, h, 0:HEAD_DIM], span, real)
+            top = jnp.max(scores, axis=0, keepdims=True)
+            expo = jnp.exp(scores - top)
+            total = jnp.sum(expo, axis=0, keepdims=True)
+            probs = (expo * (1.0 / total)).astype(BF16)
+            out = jnp.dot(value_cols, probs, preferred_element_type=F32).astype(BF16)
+            lse_ref[i, h] = top + jnp.log(total)
+            if k < 3:
+                att[i, h] = out
+                result(h, k).start()
+            else:
+                back[me, h] = out
+        return carry
+
+    lax.fori_loop(0, heads, one_head, 0)
+    qkv_ref[...] = got[...]
+    for h in range(heads):
+        for k in range(3):
+            arrival(h, k).wait_send()
+            result(h, k).wait()
+    o_ref[...] = back[...]
+
+
+def attend_forward(blocks, real):
+    shards, heads, wide, span = blocks.shape
+    vmem = pl.BlockSpec(memory_space=pltpu.VMEM)
+    small = (shards, heads, HEAD_DIM, span)
     return pl.pallas_call(
         functools.partial(attend_kernel, real),
-        grid=(heads,),
         out_shape=(
-            jax.ShapeDtypeStruct((shards, heads, HEAD_DIM, span), BF16),
+            jax.ShapeDtypeStruct(blocks.shape, BF16),
+            jax.ShapeDtypeStruct(small, BF16),
             jax.ShapeDtypeStruct((shards, heads, 1, span), F32),
         ),
-        in_specs=[head_spec(shards, span, 0), head_spec(shards, span, heads), head_spec(shards, span, 2 * heads)],
-        out_specs=(
-            head_spec(shards, span, 0),
-            pl.BlockSpec((shards, 1, 1, span), lambda h: (0, h, 0, 0)),
+        in_specs=[vmem],
+        out_specs=(vmem,) * 3,
+        scratch_shapes=[pltpu.VMEM(blocks.shape, BF16), pltpu.VMEM(small, BF16), pltpu.VMEM(small, BF16)]
+        + [pltpu.SemaphoreType.DMA((heads, 3))] * 4,
+        compiler_params=pltpu.CompilerParams(
+            collective_id=2, has_side_effects=True, vmem_limit_bytes=VMEM_BYTES
         ),
-        compiler_params=pltpu.CompilerParams(vmem_limit_bytes=VMEM_BYTES),
         name="attend_forward",
-    )(qkv, qkv, qkv)
-
-
-def attend_back_kernel(real, q_ref, k_ref, v_ref, g_ref, lse_ref, dq_ref, dk_ref, dv_ref):
-    shards, _, _, span = q_ref.shape
-    key_cols, value_cols = side_by_side(k_ref), side_by_side(v_ref)
-    grad_key, grad_value = None, None
-    for i in range(shards):
-        query, grad = q_ref[i, 0], g_ref[i, 0]
-        scores = masked_scores(key_cols, query, span, real)
-        probs = jnp.exp(scores - lse_ref[i, 0])
-        grad_probs = rows_dot(value_cols, grad)
-        inner = jnp.sum(probs * grad_probs, axis=0, keepdims=True)
-        grad_scores = (probs * (grad_probs - inner)).astype(BF16)
-        dq_ref[i, 0] = (
-            jnp.dot(key_cols, grad_scores, preferred_element_type=F32) * HEAD_DIM ** (-0.5)
-        ).astype(BF16)
-        key_part = cols_dot(query, grad_scores)
-        value_part = cols_dot(grad, probs.astype(BF16))
-        grad_key = key_part if grad_key is None else grad_key + key_part
-        grad_value = value_part if grad_value is None else grad_value + value_part
-    for i in range(shards):
-        dk_ref[i, 0] = grad_key[:, i * span : (i + 1) * span].astype(BF16)
-        dv_ref[i, 0] = grad_value[:, i * span : (i + 1) * span].astype(BF16)
-
-
-def attend_backward(qkv, grad, lse, heads, real):
-    shards, _, _, span = qkv.shape
-    lse_spec = pl.BlockSpec((shards, 1, 1, span), lambda h: (0, h, 0, 0))
-    shape = jax.ShapeDtypeStruct((shards, heads, HEAD_DIM, span), BF16)
+    )(blocks)
+
+
+def attend_back_kernel(real, g_ref, qkv_ref, lse_ref, o_ref, got, work, back, x_send, x_recv, o_send, o_recv):
+    me = lax.axis_index("seq")
+    ring = seq_ring(me)
+    shards, heads, _, span = g_ref.shape
+    greet("seq", ring)
+
+    def arrival(h, k):
+        return chunk(g_ref.at[ring[k], h], got.at[me, h], x_send.at[h, k], x_recv.at[h, k], ring[k])
+
+    def result(h, k):
+        return chunk(work.at[ring[k], h], back.at[me, h], o_send.at[h, k], o_recv.at[h, k], ring[k])
+
+    for h in range(heads):
+        for k in range(3):
+            arrival(h, k).start()
+    got[me] = g_ref[me]
+
+    def one_head(h, carry):
+        for k in range(3):
+            arrival(h, k).wait_recv()
+        key_cols, value_cols = head_cols(qkv_ref, h, HEAD_DIM), head_cols(qkv_ref, h, 2 * HEAD_DIM)
+        grad_key, grad_value = None, None
+        for i in range(shards):
+            query, grad = qkv_ref[i, h, 0:HEAD_DIM], got[i, h]
+            scores = masked_scores(key_cols, query, span, real)
+            probs = jnp.exp(scores - lse_ref[i, h])
+            grad_probs = rows_dot(value_cols, grad)
+            inner = jnp.sum(probs * grad_probs, axis=0, keepdims=True)
+            grad_scores = (probs * (grad_probs - inner)).astype(BF16)
+            work[i, h, 0:HEAD_DIM] = (
+                jnp.dot(key_cols, grad_scores, preferred_element_type=F32) * HEAD_DIM ** (-0.5)
+            ).astype(BF16)
+            key_part = cols_dot(query, grad_scores)
+            value_part = cols_dot(grad, probs.astype(BF16))
+            grad_key = key_part if grad_key is None else grad_key + key_part
+            grad_value = value_part if grad_value is None else grad_value + value_part
+        for i in range(shards):
+            piece = slice(i * span, (i + 1) * span)
+            work[i, h, HEAD_DIM : 2 * HEAD_DIM] = grad_key[:, piece].astype(BF16)
+            work[i, h, 2 * HEAD_DIM : 3 * HEAD_DIM] = grad_value[:, piece].astype(BF16)
+        for k in range(3):
+            result(h, k).start()
+        back[me, h] = work[me, h]
+        return carry
+
+    lax.fori_loop(0, heads, one_head, 0)
+    for h in range(heads):
+        for k in range(3):
+            arrival(h, k).wait_send()
+            result(h, k).wait()
+    o_ref[...] = back[...]
+
+
+def attend_backward(grad, qkv, lse, real):
+    heads = qkv.shape[1]
+    vmem = pl.BlockSpec(memory_space=pltpu.VMEM)
     return pl.pallas_call(
         functools.partial(attend_back_kernel, real),
-        grid=(heads,),
-        out_shape=(shape, shape, shape),
-        in_specs=[
-            head_spec(shards, span, 0),
-            head_spec(shards, span, heads),
-            head_spec(shards, span, 2 * heads),
-            head_spec(shards, span, 0),
-            lse_spec,
-        ],
-        out_specs=(head_spec(shards, span, 0),) * 3,
-        compiler_params=pltpu.CompilerParams(vmem_limit_bytes=VMEM_BYTES),
+        out_shape=jax.ShapeDtypeStruct(qkv.shape, BF16),
+        in_specs=[vmem] * 3,
+        out_specs=vmem,
+        scratch_shapes=[pltpu.VMEM(grad.shape, BF16), pltpu.VMEM(qkv.shape, BF16), pltpu.VMEM(qkv.shape, BF16)]
+        + [pltpu.SemaphoreType.DMA((heads, 3))] * 4,
+        compiler_params=pltpu.CompilerParams(
+            collective_id=3, has_side_effects=True, vmem_limit_bytes=VMEM_BYTES
+        ),
         name="attend_backward",
-    )(qkv, qkv, qkv, grad, lse)
-
-
-def project_kernel(rows_ref, w_ref, b_ref, o_ref):
+    )(grad, qkv, lse)
+
+
+def project_kernel(rows_ref, w_ref, b_ref, s_ref, o_ref):
     total = cols_dot(w_ref[...], rows_ref[0]) + b_ref[...]
-    width = total.shape[0] // 3
-    o_ref[0, :width] = (total[:width].astype(BF16).astype(F32) * HEAD_DIM ** (-0.5)).astype(BF16)
-    o_ref[0, width:] = total[width:].astype(BF16)
-
-
-def project(rows, w_flat, bias):
+    o_ref[0] = (total.astype(BF16).astype(F32) * s_ref[...]).astype(BF16)
+
+
+def project(rows, w_flat, bias, scale):
     clips, span, depth = rows.shape
     width = w_flat.shape[0]
     return pl.pallas_call(
@@ -460,11 +492,12 @@
             pl.BlockSpec((1, span, depth), lambda c: (c, 0, 0)),
             pl.BlockSpec((width, depth), lambda c: (0, 0)),
             pl.BlockSpec((width, 1), lambda c: (0, 0)),
+            pl.BlockSpec((width, 1), lambda c: (0, 0)),
         ],
         out_specs=pl.BlockSpec((1, width, span), lambda c: (c, 0, 0)),
         compiler_params=pltpu.CompilerParams(vmem_limit_bytes=VMEM_BYTES),
         name="project",
-    )(rows, w_flat, bias)
+    )(rows, w_flat, bias, scale)
 
 
 def layer_norm(values, gain_vec, shift_vec):
@@ -510,13 +543,15 @@
     norm_one = layer_norm(resid, gain_one, shift_one).astype(BF16)
     rows_one = gather_rows(norm_one)
     clips = rows_one.shape[0]
-    w_flat = jnp.swapaxes(w_qkv, 1, 2).reshape(3 * width, depth)
+    w_flat = w_qkv.reshape(3, depth, heads, HEAD_DIM).transpose(2, 0, 3, 1).reshape(3 * width, depth)
     bias_qv = b_query_value.astype(F32)
-    bias_three = jnp.concatenate([bias_qv[0], jnp.zeros_like(bias_qv[0]), bias_qv[1]])[:, None]
-    projected = project(rows_one, w_flat, bias_three)
-    qkv = swap_seq(projected, 2).reshape(clips, 3 * heads, HEAD_DIM, span)
-    attended, lse = attend_forward(qkv, heads, real)
-    attended = swap_seq(attended.reshape(clips, width, span), 3)
+    bias_three = jnp.stack([bias_qv[0], jnp.zeros_like(bias_qv[0]), bias_qv[1]])
+    bias_three = bias_three.reshape(3, heads, HEAD_DIM).swapaxes(0, 1).reshape(-1, 1)
+    row = jnp.arange(3 * width)[:, None]
+    scale = jnp.where(row % (3 * HEAD_DIM) < HEAD_DIM, HEAD_DIM ** (-0.5), 1.0).astype(F32)
+    projected = project(rows_one, w_flat, bias_three, scale)
+    qkv, attended, lse = attend_forward(projected.reshape(clips, heads, 3 * HEAD_DIM, span), real)
+    attended = attended.reshape(clips, width, span)
     branch_one = scatter_sum(dot("cef,ed->cfd", attended, w_out).astype(BF16))
     hidden = resid + branch_one + b_out.astype(F32)
     norm_two = layer_norm(hidden, gain_two, shift_two).astype(BF16)
@@ -537,6 +572,7 @@
     grad_up, grad_down, grad_norm_two = lax.optimization_barrier(
         (grad_up.astype(BF16), grad_down.astype(BF16), grad_norm_two)
     )
+    grad_up, grad_down = lax.psum((grad_up, grad_down), ("dp", "seq"))
     grad_norm_two = scatter_sum(grad_norm_two)
 
     _, pull_two = jax.vjp(layer_norm, hidden, gain_two, shift_two)
@@ -546,21 +582,14 @@
     grad_rows = gather_rows(hidden_low)
     grad_att = dot("cfd,ed->cef", grad_rows, w_out).astype(BF16)
     grad_out = dot("cef,cfd->ed", attended, grad_rows).astype(BF16)
-    grad_up, grad_down, grad_out, grad_att = lax.optimization_barrier((grad_up, grad_down, grad_out, grad_att))
-    grad_up, grad_down, grad_out = lax.psum((grad_up, grad_down, grad_out), ("dp", "seq"))
-    grad_att = swap_seq(grad_att, 3).reshape(clips, heads, HEAD_DIM, span)
-    grads = attend_backward(qkv, grad_att, lse, heads, real)
-    grad_qkv_cols = jnp.concatenate([g.reshape(clips, width, span) for g in grads], axis=1)
-    grad_qkv_cols = swap_seq(grad_qkv_cols, 2)
+    grads = attend_backward(grad_att.reshape(clips, heads, HEAD_DIM, span), qkv, lse, real)
+    grad_qkv_cols = grads.reshape(clips, 3 * width, span)
     grad_norm_one = dot("ckf,kd->cfd", grad_qkv_cols, w_flat).astype(BF16)
-    bias_sums = jnp.sum(grad_qkv_cols, axis=(0, 2), dtype=F32).reshape(3, width)
+    bias_sums = jnp.sum(grad_qkv_cols, axis=(0, 2), dtype=F32).reshape(heads, 3, HEAD_DIM)
     grad_qkv = dot("ckf,cfd->kd", grad_qkv_cols, rows_one).astype(BF16)
-    grad_up, grad_down, grad_out, branch_two, grad_norm_one = lax.optimization_barrier(
-        (grad_up, grad_down, grad_out, branch_two, grad_norm_one)
-    )
-    output = (hidden + branch_two.astype(F32) + b_down.astype(F32)).astype(BF16)
     seq_size = lax.axis_size("seq")
-    grad_norm_one, grad_part = scatter_both(grad_norm_one, grad_qkv.reshape(seq_size, -1, depth))
+    mine = jnp.concatenate([grad_qkv, grad_out]).reshape(seq_size, -1, depth)
+    grad_norm_one, grad_part = scatter_both(grad_norm_one, mine)
 
     _, pull_one = jax.vjp(layer_norm, resid, gain_one, shift_one)
     grad_resid, grad_gain_one, grad_shift_one = pull_one(grad_norm_one)
@@ -580,10 +609,13 @@
     vectors = jnp.swapaxes(vectors.reshape(6, parts, width), 0, 1)
     vectors = jnp.pad(vectors, ((0, 0), (0, 2), (0, lanes - width)))
     hidden_parts = grad_up_bias.reshape(-1, width)
-    local = jnp.concatenate([bias_sums[0][None], bias_sums[2][None], hidden_parts])
+    local = jnp.concatenate([bias_sums[:, 0].reshape(1, -1), bias_sums[:, 2].reshape(1, -1), hidden_parts])
     local = jnp.pad(local, ((0, 8 - local.shape[0]), (0, lanes - width)))
-    grad_qkv, small = finish(grad_part, vectors, local, lax.axis_size("dp"))
-    grad_qkv = jnp.swapaxes(grad_qkv.reshape(3, width, depth), 1, 2)
+    grad_up, grad_down, branch_two, vectors = lax.optimization_barrier((grad_up, grad_down, branch_two, vectors))
+    output = (hidden + branch_two.astype(F32) + b_down.astype(F32)).astype(BF16)
+    mine, small = finish(grad_part, vectors, local, lax.axis_size("dp"))
+    mine = mine.reshape(-1, depth)
+    grad_qkv = mine[: 3 * width].reshape(heads, 3, HEAD_DIM, depth).transpose(1, 3, 0, 2).reshape(3, depth, width)
     small = small[:, :width]
     return (
         output[None, :real],
@@ -592,7 +624,7 @@
         small[1],
         grad_qkv,
         small[8:10],
-        grad_out.astype(F32),
+        mine[3 * width :],
         small[2],
         small[3],
         small[4],

time: 499 us -> 509 us (1.020)
  waiting for transfers between devices: 38.4 us -> 71.5 us
  Pallas kernels: 341 us -> 311 us
    pallas_call x6 -> x2, Pallas kernels: 170 us -> 116 us  [the longest x1 59.2 us: attend_forward(): pl.pallas_call(functools.partial(attend_kernel, real), out_shape=(jax.Sha...]
    psum x1, waiting for transfers between devices: 38.3 us -> 71.4 us  [on_device(): grad_up, grad_down = lax.psum((grad_up, grad_down), ('dp', 'seq'))]
    pallas_call x1, Pallas kernels: 21.1 us -> 44.6 us  [scatter_both(): pl.pallas_call(scatter_both_kernel, out_shape=(jax.ShapeDtypeStruct(shape...]
  transfers between devices with their start and end apart: 3 -> 3, of which waited for: 1 -> 1; matrix products, arithmetic and copies ran while one was open for 16% -> 17% of each run, Pallas kernels for 59% -> 56%
where the time goes in v3:
time: 509 us; the launch traced here: 500 us
  Pallas kernels  311 us (61%)
  waiting for transfers between devices  71.5 us (14%)
  other arithmetic  43.8 us (9%)
  matrix products  42.3 us (8%)
  local copies, waits for them, and re-layouts  16.9 us (3%)
  between operations  14.7 us (3%)
    psum x1, waiting for transfers between devices, on_device(): grad_up, grad_down = lax.psum((grad_up, grad_down), ('dp', 'seq'))  71.4 us
    pallas_call x3, Pallas kernels, gather_rows(): pl.pallas_call(gather_kernel, out_shape=jax.ShapeDtypeStruct((4,) + block...  65.1 us
    pallas_call x1, Pallas kernels, attend_forward(): pl.pallas_call(functools.partial(attend_kernel, real), out_shape=(jax.Sha...  59.2 us
    pallas_call x1, Pallas kernels, attend_backward(): pl.pallas_call(functools.partial(attend_back_kernel, real), out_shape=jax...  57 us
    pallas_call x2, Pallas kernels, scatter_sum(): pl.pallas_call(scatter_kernel, out_shape=jax.ShapeDtypeStruct(shape, F32)...  46 us
    pallas_call x1, Pallas kernels, scatter_both(): pl.pallas_call(scatter_both_kernel, out_shape=(jax.ShapeDtypeStruct(shape...  44.6 us
    dot_general x11, matrix products, dot(): return jnp.einsum(spec, a, b, preferred_element_type=F32)  42.3 us
    pallas_call x1, Pallas kernels, finish(): pl.pallas_call(functools.partial(finish_kernel, dp_size), out_shape=(jax....  33.2 us
  transfers between devices with their start and end apart: 3, of which 1 were waited for; matrix products, arithmetic and copies ran while one was open for 17% of the time, Pallas kernels for 56%

profile of v3, /device:TPU:0, one launch (start us, length us, event | category | flops | bytes accessed | tf_op | source)
XLA Modules:
  0.0 499.9 jit_solution(5160733683810414007)
XLA Ops:
  7.3 2.0 pad.16
  11.9 25.0 %gather_rows.3.rows_ref = bf16[4,384,768]{2,1,0:T(8,128)(2,1)} custom-call(bf16[384,768]{1,0:T(8,128)(2,1)} %fusion.14.x_ref), custom_call_target="tpu_custom_call" | custom-call | tf_op jit(solution)/shard_map/gather_rows/pallas_call | solution.py:77
  39.1 5.6 %project.1 = bf16[4,576,384]{2,1,0:T(8,128)(2,1)} custom-call(bf16[4,384,768]{2,1,0:T(8,128)(2,1)} %gather_rows.3.rows_ref, bf16[576,768]{1,0:T(8,128)(2,1)} %bitcast.95, f32[576,1]{1,0:T(8,128)} %reshape.215.b_ref, f32[576,1]{1,0:T(8,128)} %fusion.37.s_ref), custom_call_target="tpu_custom_call" | custom-call | tf_op jit(solution)/shard_map/project/pallas_call | solution.py:487
  44.7 59.2 %attend_forward.1 = (bf16[4,3,192,384]{3,2,1,0:T(8,128)(2,1)}, bf16[4,3,64,384]{3,2,1,0:T(8,128)(2,1)}, f32[4,3,1,384]{3,2,1,0:T(1,128)}) custom-call(bf16[4,3,192,384]{3,2,1,0:T(8,128)(2,1)} %bitcast.93), custom_call_target="tpu_custom_call" | custom-call | tf_op jit(solution)/shard_map/attend_forward/pallas_call | solution.py:391
  104.0 3.3 convolution_convert_fusion.3.x_ref
  107.3 19.9 %scatter_sum.2 = f32[384,768]{1,0:T(8,128)} custom-call(bf16[4,384,768]{2,1,0:T(8,128)(2,1)} %convolution_convert_fusion.3.x_ref), custom_call_target="tpu_custom_call" | custom-call | tf_op jit(solution)/shard_map/scatter_sum/pallas_call | solution.py:127
  127.2 1.5 fusion.44
  130.1 20.5 %gather_rows.4 = bf16[4,384,768]{2,1,0:T(8,128)(2,1)} custom-call(bf16[384,768]{1,0:T(8,128)(2,1)} %add_convert_fusion.1.x_ref), custom_call_target="tpu_custom_call" | custom-call | tf_op jit(solution)/shard_map/gather_rows/pallas_call | solution.py:77
  150.6 4.9 fusion.25
  155.5 22.2 %multiply_convert_fusion = (bf16[4,384,768]{2,1,0:T(8,128)(2,1)S(1)}, f32[4,384,768]{2,1,0:T(8,128)}) fusion(f32[4,384,768]{2,1,0:T(8,128)S(1)} %get-tuple-element.73, f32[768]{0:T(1024)S(1)} %convert_element_type.115, u8[384,768]{1,0:T(8,128)(4,1)S(1)} %get-tuple-element.43, u8[384,768]{1,0:T(8,128)(4,1)S(1)} %get-tuple-element.42), kind=kLoop, calls=%fused_computation.8 | loop fusion | flops 83755008 | bytes 12389376 | tf_op jit(solution)/shard_map/convert_element_type | solution.py:561
  179.2 3.4 convolution_convert_fusion.1
  183.3 8.5 %convert_reduce_fusion = (f32[768]{0:T(1024)S(1)}, bf16[4,384,768]{2,1,0:T(8,128)(2,1)S(1)}) fusion(f32[4,384,768]{2,1,0:T(8,128)} %get-tuple-element.61, bf16[4,384,768]{2,1,0:T(8,128)(2,1)} %bitcast.114, bf16[768,768]{1,0:T(8,128)(2,1)} %param.25, f32[4,384,768]{2,1,0:T(8,128)} %copy-done.8, f32[768]{0:T(1024)S(1)} %convert_element_type.115), kind=kOutput, calls=%fused_computation.7 | convolution fusion | flops 1831992576 | bytes 15341568 | tf_op jit(solution)/shard_map/cfd,ed->cfe/dot_general | solution.py:514
  191.9 3.5 convolution_convert_fusion.2.x_ref
  195.4 3.1 bitcast_convert_fusion.1
  198.5 3.1 bitcast_convert_fusion
  201.6 26.1 %scatter_sum.3 = f32[384,768]{1,0:T(8,128)} custom-call(bf16[4,384,768]{2,1,0:T(8,128)(2,1)} %convolution_convert_fusion.2.x_ref), custom_call_target="tpu_custom_call" | custom-call | tf_op jit(solution)/shard_map/scatter_sum/pallas_call | solution.py:127
  227.8 1.9 multiply_reduce_fusion
  232.0 19.6 %gather_rows.5 = bf16[4,384,768]{2,1,0:T(8,128)(2,1)} custom-call(bf16[384,768]{1,0:T(8,128)(2,1)} %convert_element_type.123.x_ref), custom_call_target="tpu_custom_call" | custom-call | tf_op jit(solution)/shard_map/gather_rows/pallas_call | solution.py:77
  251.6 3.4 convolution_convert_fusion.4
  255.0 57.0 %attend_backward.1 = bf16[4,3,192,384]{3,2,1,0:T(8,128)(2,1)} custom-call(bf16[4,3,64,384]{3,2,1,0:T(8,128)(2,1)} %bitcast.101, bf16[4,3,192,384]{3,2,1,0:T(8,128)(2,1)} %get-tuple-element.32.qkv_ref, f32[4,3,1,384]{3,2,1,0:T(1,128)} %get-tuple-element.33.lse_ref), custom_call_target="tpu_custom_call" | custom-call | tf_op jit(solution)/shard_map/attend_backward/pallas_call | solution.py:465
  312.0 1.8 convert_reduce_fusion.1
  314.2 2.4 fusion.12
  316.7 3.1 bitcast_convert_fusion.2
  321.7 3.5 convolution_convert_fusion.x_ref
  325.2 44.6 %scatter_both.1 = (f32[384,768]{1,0:T(8,128)}, bf16[192,768]{1,0:T(8,128)(2,1)}) custom-call(bf16[4,384,768]{2,1,0:T(8,128)(2,1)} %convolution_convert_fusion.x_ref, bf16[4,192,768]{2,1,0:T(8,128)(2,1)} %bitcast.94), custom_call_target="tpu_custom_call" | custom-call | tf_op jit(solution)/shard_map/scatter_both/pallas_call | solution.py:196
  369.8 1.9 fusion.17
  374.9 71.4 %all-reduce.7.cloned.1.call-done = (bf16[768,768]{1,0:T(8,128)(2,1)}, bf16[768,768]{1,0:T(8,128)(2,1)}) async-done(((bf16[768,768]{1,0:T(8,128)(2,1)}, bf16[768,768]{1,0:T(8,128)(2,1)}), (bf16[768,768]{1,0:T(8,128)(2,1)}, bf16[768,768]{1,0:T(8,128)(2,1)})) %all-reduce.7.cloned.1.call-update) | async-done | bytes 2359312 | tf_op jit(solution)/shard_map/psum | solution.py:575
  446.4 33.2 %finish.1 = (f32[4,192,768]{2,1,0:T(8,128)}, f32[16,256]{1,0:T(8,128)}) custom-call(bf16[192,768]{1,0:T(8,128)(2,1)} %get-tuple-element.36.part_ref, f32[4,8,256]{2,1,0:T(8,128)} %pad.17.vec_ref, f32[8,256]{1,0:T(8,128)} %select_maximum_fusion.local_ref), custom_call_target="tpu_custom_call" | custom-call | tf_op jit(solution)/shard_map/finish/pallas_call | solution.py:288
  479.6 1.6 slice.69
  481.2 1.9 slice_bitcast_fusion
  486.2 2.8 convert_element_type.135
  489.1 1.6 convert_element_type.136
  (125 shorter events, 21.5 us)
Async XLA Ops:
  7.2 143.4 %copy-start = (bf16[768,768]{1,0:T(8,128)(2,1)S(1)}, bf16[768,768]{1,0:T(8,128)(2,1)}, u32[]{:S(2)}) copy-start(bf16[768,768]{1,0:T(8,128)(2,1)} %param.23) | copy-start | bytes 3538948
  7.2 3.0 copy-start.2
  7.2 3.5 copy-start.23
  7.2 3.5 copy-start.24
  7.2 176.1 %all-gather.3.cloned.1.call-start = ((), (), s32[]{:S(2)}) async-start(), calls=%async_computation.2 | async-start | bytes 2949120 | tf_op jit(solution)/shard_map/all_gather | solution.py:559
  9.3 365.6 %reduce-scatter.2.cloned.1.call-start = ((), (), s32[]{:S(2)}) async-start(), calls=%async_computation.1 | async-start | bytes 2949120 | tf_op jit(solution)/shard_map/reduce_scatter | solution.py:566
  10.4 26.5 %copy-start.22 = (bf16[2,192]{1,0:T(2,128)(2,1)S(1)}, bf16[2,192]{1,0:T(2,128)(2,1)}, u32[]{:S(2)}) copy-start(bf16[2,192]{1,0:T(2,128)(2,1)} %param.18) | copy-start | bytes 2308
  10.7 27.4 %copy-start.17 = (bf16[3,768,192]{1,2,0:T(8,128)(2,1)S(1)}, bf16[3,768,192]{1,2,0:T(8,128)(2,1)}, u32[]{:S(2)}) copy-start(bf16[3,768,192]{1,2,0:T(8,128)(2,1)} %param.17) | copy-start | bytes 2654212
  39.1 64.8 %copy-start.20 = (bf16[192,768]{1,0:T(8,128)(2,1)S(1)}, bf16[192,768]{1,0:T(8,128)(2,1)}, u32[]{:S(2)}) copy-start(bf16[192,768]{1,0:T(8,128)(2,1)} %param.19) | copy-start | bytes 884740
  107.3 19.9 %copy-start.25 = (bf16[768]{0:T(1024)(128)(2,1)S(1)}, bf16[768]{0:T(1024)(128)(2,1)}, u32[]{:S(2)}) copy-start(bf16[768]{0:T(1024)(128)(2,1)} %param.20) | copy-start | bytes 4612
  127.2 1.8 copy-start.26
  127.2 1.8 copy-start.27
  129.0 21.6 %copy-start.28 = (bf16[768]{0:T(1024)(128)(2,1)S(1)}, bf16[768]{0:T(1024)(128)(2,1)}, u32[]{:S(2)}) copy-start(bf16[768]{0:T(1024)(128)(2,1)} %param.24) | copy-start | bytes 4612
  155.5 22.3 %copy-start.8 = (f32[4,384,768]{2,1,0:T(8,128)}, f32[4,384,768]{2,1,0:T(8,128)S(1)}, u32[]{:S(2)}) copy-start(f32[4,384,768]{2,1,0:T(8,128)S(1)} %get-tuple-element.73) | copy-start | bytes 14155780
  155.5 23.7 %copy-start.31 = (bf16[768,768]{1,0:T(8,128)(2,1)S(1)}, bf16[768,768]{1,0:T(8,128)(2,1)}, u32[]{:S(2)}) copy-start(bf16[768,768]{1,0:T(8,128)(2,1)} %param.25) | copy-start | bytes 3538948
  182.7 263.7 %all-reduce.7.cloned.1.call-start = ((), (), s32[]{:S(2)}) async-start(), calls=%async_computation.3 | async-start | bytes 4718592 | tf_op jit(solution)/shard_map/psum | solution.py:575
  191.9 3.5 copy-start.12
  195.4 3.1 copy-start.14
  195.4 3.1 copy-start.30
  227.8 1.9 copy-start.3
  231.0 20.6 %copy-start.4 = (f32[384,768]{1,0:T(8,128)}, f32[384,768]{1,0:T(8,128)S(1)}, u32[]{:S(2)}) copy-start(f32[384,768]{1,0:T(8,128)S(1)} %get-tuple-element.57) | copy-start | bytes 3538948
  312.0 2.2 copy-start.18
  314.2 2.5 copy-start.6
  316.7 4.2 copy-start.11
  319.8 1.9 copy-start.7
  369.8 3.7 copy-start.9
  479.5 3.5 copy-start.21
  485.6 3.5 copy-start.16
  489.1 1.7 copy-start.5
  489.1 2.5 copy-start.10
  489.1 2.6 copy-start.19
  490.7 2.3 copy-start.1
  (3 other events, 3.2 us)
Sparse Core Ops, SparseCore 0:
  10.2 32.9 all-gather.2
  182.8 39.3 reduce-scatter.1
  314.1 132.2 all-reduce.6
